TPU v7x, 128 devices: a whole 4x4x4 slice. The times are simulated.
128 devices in a mesh: prow: 8 (over x, core), pcol: 16 (over z, y).
Axes of the slice: x: 4, y: 4, z: 4, core: 2. Of those that a mesh axis runs over, the one named last changes fastest.
Arguments:
- pivot_inverse: bfloat16 [4, 256, 256], P(None, None, 'prow'), may hold values from -0.375 to 0.375
- upper_block: bfloat16 [4, 256, 8192], P(None, 'prow', 'pcol'), may hold values from -6 to 6
- lower_panel: bfloat16 [4, 256, 8192], P(None, 'pcol', 'prow'), may hold values from -0.375 to 0.375
- update_block: bfloat16 [4, 8192, 8192], P(None, 'prow', 'pcol'), may hold values from -6 to 6
- row_map: int32 [4, 64], P(None, 'prow'), may hold values from 0 to 127, as said below
- column_map: int32 [4, 64], P(None, 'pcol'), may hold values from 0 to 127, as said below
- parent_front: float32 [16384, 16384], P('prow', 'pcol'), may hold values from -6 to 6
Outputs:
- assembled: float32 [16384, 16384], P('prow', 'pcol')
Inputs may be any that keep to these rules, and one draw needn't show every extreme that they name: `row_map`: entries of one front are distinct. Ancestor row tile p belongs to prow index p // 16. Of the 8 row tiles that one prow index holds of a front, at most 2 go to one prow index. At most 10 row tiles of one front go to one prow index. `column_map`: entries of one front are distinct. Ancestor column tile p belongs to pcol index p // 8. The 4 column tiles that pcol index c holds of a front go to indices c to c + 3, counted modulo the number of pcol indices, at most 2 to one index.
All inputs are finite; a program needn't handle non-finite values.
Results may differ from a plain program's by a relative error of at most 0.0027.
Values may be sent and summed in bfloat16 or wider, within the bound.
A program may use at most 192 MiB of HBM per device.

v0:
```python
import jax
import jax.numpy as jnp
from jax import lax
from jax.sharding import PartitionSpec as P

TILE = 128
REACH = 4


def shifted(array, axis, by):
    peers = lax.axis_size(axis)
    return lax.ppermute(array, axis, [(i, (i + by) % peers) for i in range(peers)])


def earlier_same(values):
    count = values.shape[0]
    steps = jnp.arange(count, dtype=jnp.int32)
    same = (values[:, None] == values[None, :]) & (steps[None, :] < steps[:, None])
    return jnp.sum(same.astype(jnp.int32), axis=1)


def pack_columns(pieces, offsets, send_rank, place_slot, wanted, col_cap):
    slots = jnp.arange(col_cap, dtype=jnp.int32)
    select = jnp.concatenate(
        [(offsets[None, :] == want) & (send_rank[None, :] == slots[:, None]) for want in wanted],
        axis=0,
    )
    packed = jnp.einsum(
        "rkv,ck->rcv", pieces, select.astype(jnp.bfloat16), preferred_element_type=jnp.float32
    ).astype(jnp.bfloat16)
    tile_label = jnp.sum(select.astype(jnp.int32) * (place_slot + 1)[None, :], axis=1) - 1
    return (packed, tile_label)


def per_device(
    pivot_inverse, upper_block, lower_panel, update_block, row_map, column_map, parent_front
):
    row_shards = lax.axis_size("prow")
    col_shards = lax.axis_size("pcol")
    col_index = lax.axis_index("pcol")
    assembled = parent_front
    owner_rows = parent_front.shape[0] // TILE
    owner_cols = parent_front.shape[1] // TILE
    for front_index in range(update_block.shape[0]):
        partial_panel = jnp.dot(
            pivot_inverse[front_index], upper_block[front_index], preferred_element_type=jnp.float32
        )
        solved = lax.psum(partial_panel, "prow")
        solved = solved.astype(jnp.bfloat16)
        complement = (
            update_block[front_index].astype(jnp.float32)
            - lax.dot_general(
                lax.all_gather(lower_panel[front_index], "pcol", axis=0, tiled=True),
                solved,
                (((0,), (0,)), ((), ())),
                preferred_element_type=jnp.float32,
            )
        ).astype(jnp.bfloat16)
        row_tiles = complement.shape[0] // TILE
        width = complement.shape[1]
        row_cap = 2 * row_tiles // row_shards
        recv_cap = row_tiles + row_cap
        targets = row_map[front_index]
        owner_index = targets // owner_rows
        place_slot = targets % owner_rows
        send_rank = earlier_same(owner_index)
        owners = jnp.arange(row_shards, dtype=jnp.int32)
        slots = jnp.arange(row_cap, dtype=jnp.int32)
        select = (owner_index[None, None, :] == owners[:, None, None]) & (
            send_rank[None, None, :] == slots[None, :, None]
        )
        pieces = complement.reshape(row_tiles, TILE, width)
        outgoing = jnp.einsum(
            "dck,kuv->dcuv", select.astype(jnp.bfloat16), pieces, preferred_element_type=jnp.float32
        ).astype(jnp.bfloat16)
        tile_label = jnp.sum(select.astype(jnp.int32) * (place_slot + 1)[None, None, :], axis=2) - 1
        received, received_label = (
            lax.all_to_all(outgoing, "prow", split_axis=0, concat_axis=0, tiled=True),
            lax.all_to_all(tile_label, "prow", split_axis=0, concat_axis=0, tiled=True),
        )
        received = received.reshape(row_shards * row_cap, TILE, width)
        received_label = received_label.reshape(row_shards * row_cap)
        valid = (received_label >= 0).astype(jnp.int32)
        compact_rank = jnp.cumsum(valid) - valid
        compact_select = (valid[None, :] == 1) & (
            compact_rank[None, :] == jnp.arange(recv_cap, dtype=jnp.int32)[:, None]
        )
        arranged = jnp.einsum(
            "qs,suv->quv",
            compact_select.astype(jnp.bfloat16),
            received,
            preferred_element_type=jnp.float32,
        ).astype(jnp.bfloat16)
        arranged_label = (
            jnp.sum(compact_select.astype(jnp.int32) * (received_label + 1)[None, :], axis=1) - 1
        )
        arranged_rows = recv_cap * TILE
        col_tiles = width // TILE
        col_cap = col_tiles // 2
        col_targets = column_map[front_index]
        col_owner = col_targets // owner_cols
        offsets = (col_owner - col_index) % col_shards
        col_place = col_targets % owner_cols
        col_rank = earlier_same(offsets)
        col_pieces = arranged.reshape(arranged_rows, col_tiles, TILE)
        arrived = [pack_columns(col_pieces, offsets, col_rank, col_place, [0], col_cap)]
        for offset in range(1, REACH):
            packed, packed_label = pack_columns(
                col_pieces, offsets, col_rank, col_place, [offset], col_cap
            )
            arrived.append(shifted((packed, packed_label), "pcol", offset))
        gathered = jnp.concatenate([item[0] for item in arrived], axis=1)
        gathered_label = jnp.concatenate([item[1] for item in arrived], axis=0)
        column_place = (
            gathered_label[:, None] == jnp.arange(owner_cols, dtype=jnp.int32)[None, :]
        ).astype(jnp.bfloat16)
        addition = jnp.einsum(
            "rsv,sq->rqv", gathered, column_place, preferred_element_type=jnp.float32
        ).astype(jnp.bfloat16)
        addition = addition.reshape(recv_cap, TILE, owner_cols * TILE)
        row_place = (
            arranged_label[None, :] == jnp.arange(owner_rows, dtype=jnp.int32)[:, None]
        ).astype(jnp.bfloat16)
        placed = jnp.einsum("qs,suv->quv", row_place, addition, preferred_element_type=jnp.float32)
        assembled = assembled + placed.reshape(owner_rows * TILE, owner_cols * TILE)
    return assembled


def solution(mesh):
    in_specs = (
        P(None, None, "prow"),
        P(None, "prow", "pcol"),
        P(None, "pcol", "prow"),
        P(None, "prow", "pcol"),
        P(None, "prow"),
        P(None, "pcol"),
        P("prow", "pcol"),
    )
    out_specs = P("prow", "pcol")
    return jax.shard_map(
        per_device, mesh=mesh, in_specs=in_specs, out_specs=out_specs, check_vma=False
    )
```

profile of v0, /device:TPU:1, one launch (start us, length us, event | category | flops | bytes accessed | tf_op | source)
XLA Modules:
  0.0 581.8 jit_solution(16150681569327582691)
XLA Ops:
  3.6 5.8 all-to-all-start.6
  40.9 20.3 %all-gather = bf16[1,256,1024]{2,1,0:T(8,128)(2,1)} all-gather(bf16[1,16,1024]{2,1,0:T(8,128)(2,1)S(1)} %get-tuple-element.61), channel_id=2, replica_groups=mesh['prow'=8,'pcol'=16] {'pcol'}, dimensions={1}, use_global_device_ids=true | all-gather | bytes 557056 | tf_op jit(solution)/shard_map/all_gather | solution.py:53
  61.2 19.2 %all-gather.1 = bf16[1,256,1024]{2,1,0:T(8,128)(2,1)} all-gather(bf16[1,16,1024]{2,1,0:T(8,128)(2,1)S(1)} %get-tuple-element.62), channel_id=3, replica_groups=mesh['prow'=8,'pcol'=16] {'pcol'}, dimensions={1}, use_global_device_ids=true | all-gather | bytes 557056 | tf_op jit(solution)/shard_map/all_gather | solution.py:53
  80.5 19.2 %all-gather.3 = bf16[1,256,1024]{2,1,0:T(8,128)(2,1)} all-gather(bf16[1,16,1024]{2,1,0:T(8,128)(2,1)S(1)} %get-tuple-element.63), channel_id=5, replica_groups=mesh['prow'=8,'pcol'=16] {'pcol'}, dimensions={1}, use_global_device_ids=true | all-gather | bytes 557056 | tf_op jit(solution)/shard_map/all_gather | solution.py:53
  99.7 19.4 %all-gather.2 = bf16[1,256,1024]{2,1,0:T(8,128)(2,1)} all-gather(bf16[1,16,1024]{2,1,0:T(8,128)(2,1)S(1)} %get-tuple-element.64), channel_id=4, replica_groups=mesh['prow'=8,'pcol'=16] {'pcol'}, dimensions={1}, use_global_device_ids=true | all-gather | bytes 557056 | tf_op jit(solution)/shard_map/all_gather | solution.py:53
  123.5 74.9 %all-reduce.2 = (bf16[256,512]{1,0:T(8,128)(2,1)S(1)}, bf16[256,512]{1,0:T(8,128)(2,1)}, bf16[256,512]{1,0:T(8,128)(2,1)}, bf16[256,512]{1,0:T(8,128)(2,1)S(1)}) all-reduce(f32[256,512]{1,0:T(8,128)} %fusion.104, f32[256,512]{1,0:T(8,128)} %fusion.106, f32[256,512]{1,0:T(8,128)} %fusion.108, ...), channel_id=1, replica_groups=mesh['prow'=8,'pcol'=16] {'prow'}, use_global_device_ids=true, to_apply=%region_39.40 | all-reduce | flops 524288 | bytes 3145728 | tf_op jit(solution)/shard_map/psum | solution.py:48
  221.2 5.7 all-to-all-start.4
  231.5 5.5 all-to-all-start.2
  241.9 5.6 all-to-all-start
  247.6 4.5 all-to-all-done
  256.8 25.8 %all-to-all-done.1 = bf16[8,2,128,512]{3,2,1,0:T(8,128)(2,1)S(1)} async-done(((bf16[8,2,128,512]{3,2,1,0:T(8,128)(2,1)}), bf16[8,2,128,512]{3,2,1,0:T(8,128)(2,1)S(1)}, u32[]{:S(2)}, u32[]{:S(2)}) %all-to-all-start.1) | async-done | bytes 2097184 | tf_op jit(solution)/shard_map/all_to_all | solution.py:78
  282.6 5.1 all-to-all-start.5
  289.7 24.5 %all-to-all-done.5 = bf16[8,2,128,512]{3,2,1,0:T(8,128)(2,1)} async-done(((bf16[8,2,128,512]{3,2,1,0:T(8,128)(2,1)}), bf16[8,2,128,512]{3,2,1,0:T(8,128)(2,1)}, u32[]{:S(2)}, u32[]{:S(2)}) %all-to-all-start.5) | async-done | bytes 2097184 | tf_op jit(solution)/shard_map/all_to_all | solution.py:78
  314.2 5.1 all-to-all-start.3
  345.8 4.4 all-to-all-start.7
  367.4 9.2 %all-to-all-done.7 = bf16[8,2,128,512]{3,2,1,0:T(8,128)(2,1)S(1)} async-done(((bf16[8,2,128,512]{3,2,1,0:T(8,128)(2,1)}), bf16[8,2,128,512]{3,2,1,0:T(8,128)(2,1)S(1)}, u32[]{:S(2)}, u32[]{:S(2)}) %all-to-all-start.7) | async-done | bytes 2097184 | tf_op jit(solution)/shard_map/all_to_all | solution.py:78
  392.6 6.0 %convert_bitcast_fusion.3 = bf16[1280,8,128]{2,1,0:T(8,128)(2,1)} fusion(bf16[1280,2,128]{2,1,0:T(2,128)(2,1)} %collective-permute-done.5, bf16[1280,2,128]{2,1,0:T(2,128)(2,1)} %collective-permute-done.4, bf16[1280,2,128]{2,1,0:T(2,128)(2,1)} %collective-permute-done.3, bf16[1280,2,128]{2,1,0:T(2,128)(2,1)S(1)} %copy-done.18, s32[8]{0:T(128)S(1)} %pad_add_fusion), kind=kOutput, calls=%fused_computation.47 | convolution fusion | flops 32768064 | bytes 5242912 | tf_op jit(solution)/shard_map/rsv,sq->rqv/dot_general | solution.py:117
  403.3 29.4 %collective-permute-done.17 = bf16[1280,2,128]{2,1,0:T(2,128)(2,1)} collective-permute-done((bf16[1280,2,128]{2,1,0:T(2,128)(2,1)}, bf16[1280,2,128]{2,1,0:T(2,128)(2,1)}, u32[]{:S(2)}, u32[]{:S(2)}) %collective-permute-start.17) | collective-permute-done | bytes 655392 | tf_op jit(solution)/shard_map/ppermute | solution.py:12
  432.7 12.6 %collective-permute-done.9 = bf16[1280,2,128]{2,1,0:T(2,128)(2,1)} collective-permute-done((bf16[1280,2,128]{2,1,0:T(2,128)(2,1)}, bf16[1280,2,128]{2,1,0:T(2,128)(2,1)}, u32[]{:S(2)}, u32[]{:S(2)}) %collective-permute-start.9) | collective-permute-done | bytes 655392 | tf_op jit(solution)/shard_map/ppermute | solution.py:12
  445.7 6.2 %convert_bitcast_fusion.1 = bf16[1280,8,128]{2,1,0:T(8,128)(2,1)} fusion(bf16[1280,2,128]{2,1,0:T(2,128)(2,1)} %collective-permute-done.17, bf16[1280,2,128]{2,1,0:T(2,128)(2,1)} %collective-permute-done.16, bf16[1280,2,128]{2,1,0:T(2,128)(2,1)} %collective-permute-done.15, bf16[1280,2,128]{2,1,0:T(2,128)(2,1)} %fusion.84, s32[8]{0:T(128)S(1)} %pad_add_fusion.2), kind=kOutput, calls=%fused_computation.45 | convolution fusion | flops 32768064 | bytes 5242912 | tf_op jit(solution)/shard_map/rsv,sq->rqv/dot_general | solution.py:117
  451.9 5.2 reshape.1088
  457.1 22.4 %collective-permute-done.11 = bf16[1280,2,128]{2,1,0:T(2,128)(2,1)} collective-permute-done((bf16[1280,2,128]{2,1,0:T(2,128)(2,1)S(1)}, bf16[1280,2,128]{2,1,0:T(2,128)(2,1)}, u32[]{:S(2)}, u32[]{:S(2)}) %collective-permute-start.11) | collective-permute-done | bytes 655392 | tf_op jit(solution)/shard_map/ppermute | solution.py:12
  479.5 6.2 %convert_bitcast_fusion.2 = bf16[1280,8,128]{2,1,0:T(8,128)(2,1)} fusion(bf16[1280,2,128]{2,1,0:T(2,128)(2,1)} %collective-permute-done.11, bf16[1280,2,128]{2,1,0:T(2,128)(2,1)} %collective-permute-done.10, bf16[1280,2,128]{2,1,0:T(2,128)(2,1)} %collective-permute-done.9, bf16[1280,2,128]{2,1,0:T(2,128)(2,1)} %fusion.80, s32[8]{0:T(128)S(1)} %pad_add_fusion.1), kind=kOutput, calls=%fused_computation.46 | convolution fusion | flops 32768064 | bytes 5242912 | tf_op jit(solution)/shard_map/rsv,sq->rqv/dot_general | solution.py:117
  485.7 5.3 reshape.1082
  491.0 16.1 %collective-permute-done.23 = bf16[1280,2,128]{2,1,0:T(2,128)(2,1)} collective-permute-done((bf16[1280,2,128]{2,1,0:T(2,128)(2,1)}, bf16[1280,2,128]{2,1,0:T(2,128)(2,1)}, u32[]{:S(2)}, u32[]{:S(2)}) %collective-permute-start.23) | collective-permute-done | bytes 655392 | tf_op jit(solution)/shard_map/ppermute | solution.py:12
  507.1 6.0 %convert_bitcast_fusion = bf16[1280,8,128]{2,1,0:T(8,128)(2,1)} fusion(bf16[1280,2,128]{2,1,0:T(2,128)(2,1)} %collective-permute-done.23, bf16[1280,2,128]{2,1,0:T(2,128)(2,1)} %collective-permute-done.22, bf16[1280,2,128]{2,1,0:T(2,128)(2,1)} %collective-permute-done.21, bf16[1280,2,128]{2,1,0:T(2,128)(2,1)S(1)} %copy-done.19, s32[8]{0:T(128)S(1)} %pad_add_fusion.3), kind=kOutput, calls=%fused_computation.44 | convolution fusion | flops 32768064 | bytes 5242912 | tf_op jit(solution)/shard_map/rsv,sq->rqv/dot_general | solution.py:117
  513.2 5.4 reshape.1094
  522.5 8.1 %copy.151 = f32[16,128,1024]{2,1,0:T(8,128)} copy(f32[16,128,1024]{2,0,1:T(8,128)S(1)} %fusion) | data formatting | bytes 16777216 | tf_op jit(solution)/shard_map/qs,suv->quv/dot_general | solution.py:124
  532.7 8.3 %copy.133 = f32[16,128,1024]{2,1,0:T(8,128)} copy(f32[16,128,1024]{2,0,1:T(8,128)S(1)} %fusion.4) | data formatting | bytes 16777216 | tf_op jit(solution)/shard_map/qs,suv->quv/dot_general | solution.py:124
  543.2 8.1 %copy.142 = f32[16,128,1024]{2,1,0:T(8,128)} copy(f32[16,128,1024]{2,0,1:T(8,128)S(1)} %fusion.2) | data formatting | bytes 16777216 | tf_op jit(solution)/shard_map/qs,suv->quv/dot_general | solution.py:124
  553.4 8.3 %copy.124 = f32[16,128,1024]{2,1,0:T(8,128)} copy(f32[16,128,1024]{2,0,1:T(8,128)S(1)} %fusion.6) | data formatting | bytes 16777216 | tf_op jit(solution)/shard_map/qs,suv->quv/dot_general | solution.py:124
  561.7 19.6 %bitcast_add_fusion = f32[2048,1024]{1,0:T(8,128)} fusion(f32[16,128,1024]{2,1,0:T(8,128)} %copy.151, f32[16,128,1024]{2,1,0:T(8,128)} %copy.142, f32[16,128,1024]{2,1,0:T(8,128)} %copy.133, f32[2048,1024]{1,0:T(8,128)} %param.13, f32[16,128,1024]{2,1,0:T(8,128)} %copy.124), kind=kLoop, calls=%fused_computation | loop fusion | flops 8388608 | bytes 50331648 | tf_op jit(solution)/shard_map/add | solution.py:125
  (252 shorter events, 153.1 us)
Async XLA Ops:
  3.6 217.6 %all-to-all-start.6 = ((s32[8,1,2]{2,1,0:T(1,128)}), s32[8,1,2]{2,1,0:T(1,128)S(1)}, u32[]{:S(2)}, u32[]{:S(2)}) async-start(s32[8,1,2]{2,1,0:T(1,128)} %copy.143), calls=%async_computation.6 | async-start | bytes 8192 | tf_op jit(solution)/shard_map/all_to_all | solution.py:79
  13.2 213.7 %collective-permute-start.6 = (s32[2]{0:T(128)}, s32[2]{0:T(128)S(1)}, u32[]{:S(2)}, u32[]{:S(2)}) collective-permute-start(s32[2]{0:T(128)} %broadcast_add_fusion.10), channel_id=1, source_target_pairs={{0,1},{1,2},{2,3},{3,4},{4,5},{5,6},{6,7},{7,8},{8,9},{9,10},{10,1... | collective-permute-start | bytes 32 | tf_op jit(solution)/shard_map/ppermute | solution.py:12
  15.1 212.1 %collective-permute-start.7 = (s32[2]{0:T(128)}, s32[2]{0:T(128)S(1)}, u32[]{:S(2)}, u32[]{:S(2)}) collective-permute-start(s32[2]{0:T(128)} %broadcast_add_fusion.9), channel_id=1, source_target_pairs={{0,2},{1,3},{2,4},{3,5},{4,6},{5,7},{6,8},{7,9},{8,10},{9,11},{10,... | collective-permute-start | bytes 32 | tf_op jit(solution)/shard_map/ppermute | solution.py:12
  18.3 210.1 %collective-permute-start.8 = (s32[2]{0:T(128)}, s32[2]{0:T(128)S(1)}, u32[]{:S(2)}, u32[]{:S(2)}) collective-permute-start(s32[2]{0:T(128)} %broadcast_add_fusion.8), channel_id=1, source_target_pairs={{0,3},{1,4},{2,5},{3,6},{4,7},{5,8},{6,9},{7,10},{8,11},{9,12},{10... | collective-permute-start | bytes 32 | tf_op jit(solution)/shard_map/ppermute | solution.py:12
  21.2 215.7 %collective-permute-start.2 = (s32[2]{0:T(128)}, s32[2]{0:T(128)S(1)}, u32[]{:S(2)}, u32[]{:S(2)}) collective-permute-start(s32[2]{0:T(128)} %broadcast_add_fusion.12), channel_id=1, source_target_pairs={{0,3},{1,4},{2,5},{3,6},{4,7},{5,8},{6,9},{7,10},{8,11},{9,12},{10... | collective-permute-start | bytes 32 | tf_op jit(solution)/shard_map/ppermute | solution.py:12
  22.7 215.1 %collective-permute-start.1 = (s32[2]{0:T(128)}, s32[2]{0:T(128)S(1)}, u32[]{:S(2)}, u32[]{:S(2)}) collective-permute-start(s32[2]{0:T(128)} %broadcast_add_fusion.13), channel_id=1, source_target_pairs={{0,2},{1,3},{2,4},{3,5},{4,6},{5,7},{6,8},{7,9},{8,10},{9,11},{10,... | collective-permute-start | bytes 32 | tf_op jit(solution)/shard_map/ppermute | solution.py:12
  221.2 10.2 %all-to-all-start.4 = ((s32[8,1,2]{2,1,0:T(1,128)}), s32[8,1,2]{2,1,0:T(1,128)S(1)}, u32[]{:S(2)}, u32[]{:S(2)}) async-start(s32[8,1,2]{2,1,0:T(1,128)} %copy.134), calls=%async_computation.4 | async-start | bytes 8192 | tf_op jit(solution)/shard_map/all_to_all | solution.py:79
  226.9 11.0 %collective-permute-start = (s32[2]{0:T(128)S(1)}, s32[2]{0:T(128)S(1)}, u32[]{:S(2)}, u32[]{:S(2)}) collective-permute-start(s32[2]{0:T(128)S(1)} %copy-done.17), channel_id=1, source_target_pairs={{0,1},{1,2},{2,3},{3,4},{4,5},{5,6},{6,7},{7,8},{8,9},{9,10},{10,1... | collective-permute-start | bytes 32 | tf_op jit(solution)/shard_map/ppermute | solution.py:12
  227.2 20.3 %collective-permute-start.18 = (s32[2]{0:T(128)S(1)}, s32[2]{0:T(128)S(1)}, u32[]{:S(2)}, u32[]{:S(2)}) collective-permute-start(s32[2]{0:T(128)S(1)} %copy-done.16), channel_id=1, source_target_pairs={{0,1},{1,2},{2,3},{3,4},{4,5},{5,6},{6,7},{7,8},{8,9},{9,10},{10,1... | collective-permute-start | bytes 32 | tf_op jit(solution)/shard_map/ppermute | solution.py:12
  228.4 27.9 %collective-permute-start.19 = (s32[2]{0:T(128)S(1)}, s32[2]{0:T(128)S(1)}, u32[]{:S(2)}, u32[]{:S(2)}) collective-permute-start(s32[2]{0:T(128)S(1)} %copy-done.15), channel_id=1, source_target_pairs={{0,2},{1,3},{2,4},{3,5},{4,6},{5,7},{6,8},{7,9},{8,10},{9,11},{10,... | collective-permute-start | bytes 32 | tf_op jit(solution)/shard_map/ppermute | solution.py:12
  231.5 10.4 %all-to-all-start.2 = ((s32[8,1,2]{2,1,0:T(1,128)}), s32[8,1,2]{2,1,0:T(1,128)S(1)}, u32[]{:S(2)}, u32[]{:S(2)}) async-start(s32[8,1,2]{2,1,0:T(1,128)} %copy.125), calls=%async_computation.2 | async-start | bytes 8192 | tf_op jit(solution)/shard_map/all_to_all | solution.py:79
  237.0 19.3 %collective-permute-start.20 = (s32[2]{0:T(128)S(1)}, s32[2]{0:T(128)S(1)}, u32[]{:S(2)}, u32[]{:S(2)}) collective-permute-start(s32[2]{0:T(128)S(1)} %copy-done.14), channel_id=1, source_target_pairs={{0,3},{1,4},{2,5},{3,6},{4,7},{5,8},{6,9},{7,10},{8,11},{9,12},{10... | collective-permute-start | bytes 32 | tf_op jit(solution)/shard_map/ppermute | solution.py:12
  237.8 18.6 %collective-permute-start.14 = (s32[2]{0:T(128)S(1)}, s32[2]{0:T(128)S(1)}, u32[]{:S(2)}, u32[]{:S(2)}) collective-permute-start(s32[2]{0:T(128)S(1)} %copy-done.13), channel_id=1, source_target_pairs={{0,3},{1,4},{2,5},{3,6},{4,7},{5,8},{6,9},{7,10},{8,11},{9,12},{10... | collective-permute-start | bytes 32 | tf_op jit(solution)/shard_map/ppermute | solution.py:12
  237.9 18.5 %collective-permute-start.13 = (s32[2]{0:T(128)S(1)}, s32[2]{0:T(128)S(1)}, u32[]{:S(2)}, u32[]{:S(2)}) collective-permute-start(s32[2]{0:T(128)S(1)} %copy-done.12), channel_id=1, source_target_pairs={{0,2},{1,3},{2,4},{3,5},{4,6},{5,7},{6,8},{7,9},{8,10},{9,11},{10,... | collective-permute-start | bytes 32 | tf_op jit(solution)/shard_map/ppermute | solution.py:12
  241.9 10.2 %all-to-all-start = ((s32[8,1,2]{2,1,0:T(1,128)}), s32[8,1,2]{2,1,0:T(1,128)S(1)}, u32[]{:S(2)}, u32[]{:S(2)}) async-start(s32[8,1,2]{2,1,0:T(1,128)} %copy.116), calls=%async_computation | async-start | bytes 8192 | tf_op jit(solution)/shard_map/all_to_all | solution.py:79
  247.5 8.9 %collective-permute-start.12 = (s32[2]{0:T(128)S(1)}, s32[2]{0:T(128)S(1)}, u32[]{:S(2)}, u32[]{:S(2)}) collective-permute-start(s32[2]{0:T(128)S(1)} %copy-done.11), channel_id=1, source_target_pairs={{0,1},{1,2},{2,3},{3,4},{4,5},{5,6},{6,7},{7,8},{8,9},{9,10},{10,1... | collective-permute-start | bytes 32 | tf_op jit(solution)/shard_map/ppermute | solution.py:12
  252.1 30.6 %all-to-all-start.1 = ((bf16[8,2,128,512]{3,2,1,0:T(8,128)(2,1)}), bf16[8,2,128,512]{3,2,1,0:T(8,128)(2,1)S(1)}, u32[]{:S(2)}, u32[]{:S(2)}) async-start(bf16[8,2,128,512]{3,2,1,0:T(8,128)(2,1)} %copy.120), calls=%async_computation.1 | async-start | bytes 4194304 | tf_op jit(solution)/shard_map/all_to_all | solution.py:78
  282.6 31.6 %all-to-all-start.5 = ((bf16[8,2,128,512]{3,2,1,0:T(8,128)(2,1)}), bf16[8,2,128,512]{3,2,1,0:T(8,128)(2,1)}, u32[]{:S(2)}, u32[]{:S(2)}) async-start(bf16[8,2,128,512]{3,2,1,0:T(8,128)(2,1)} %copy.138), calls=%async_computation.5 | async-start | bytes 4194304 | tf_op jit(solution)/shard_map/all_to_all | solution.py:78
  314.2 31.6 %all-to-all-start.3 = ((bf16[8,2,128,512]{3,2,1,0:T(8,128)(2,1)}), bf16[8,2,128,512]{3,2,1,0:T(8,128)(2,1)}, u32[]{:S(2)}, u32[]{:S(2)}) async-start(bf16[8,2,128,512]{3,2,1,0:T(8,128)(2,1)} %copy.129), calls=%async_computation.3 | async-start | bytes 4194304 | tf_op jit(solution)/shard_map/all_to_all | solution.py:78
  323.4 59.2 %collective-permute-start.3 = (bf16[1280,2,128]{2,1,0:T(2,128)(2,1)}, bf16[1280,2,128]{2,1,0:T(2,128)(2,1)}, u32[]{:S(2)}, u32[]{:S(2)}) collective-permute-start(bf16[1280,2,128]{2,1,0:T(2,128)(2,1)} %fusion.77), channel_id=1, source_target_pairs={{0,1},{1,2},{2,3},{3,4},{4,5},{5,6},{6,7},{7,8},{8,9},{9,10},{10,1... | collective-permute-start | bytes 1966088 | tf_op jit(solution)/shard_map/ppermute | solution.py:12
  325.2 59.8 %collective-permute-start.4 = (bf16[1280,2,128]{2,1,0:T(2,128)(2,1)}, bf16[1280,2,128]{2,1,0:T(2,128)(2,1)}, u32[]{:S(2)}, u32[]{:S(2)}) collective-permute-start(bf16[1280,2,128]{2,1,0:T(2,128)(2,1)} %fusion.78), channel_id=1, source_target_pairs={{0,2},{1,3},{2,4},{3,5},{4,6},{5,7},{6,8},{7,9},{8,10},{9,11},{10,... | collective-permute-start | bytes 1966088 | tf_op jit(solution)/shard_map/ppermute | solution.py:12
  329.3 59.2 %collective-permute-start.5 = (bf16[1280,2,128]{2,1,0:T(2,128)(2,1)}, bf16[1280,2,128]{2,1,0:T(2,128)(2,1)}, u32[]{:S(2)}, u32[]{:S(2)}) collective-permute-start(bf16[1280,2,128]{2,1,0:T(2,128)(2,1)} %fusion.79), channel_id=1, source_target_pairs={{0,3},{1,4},{2,5},{3,6},{4,7},{5,8},{6,9},{7,10},{8,11},{9,12},{10... | collective-permute-start | bytes 1966088 | tf_op jit(solution)/shard_map/ppermute | solution.py:12
  338.6 52.7 %collective-permute-start.15 = (bf16[1280,2,128]{2,1,0:T(2,128)(2,1)}, bf16[1280,2,128]{2,1,0:T(2,128)(2,1)}, u32[]{:S(2)}, u32[]{:S(2)}) collective-permute-start(bf16[1280,2,128]{2,1,0:T(2,128)(2,1)} %fusion.85), channel_id=1, source_target_pairs={{0,1},{1,2},{2,3},{3,4},{4,5},{5,6},{6,7},{7,8},{8,9},{9,10},{10,1... | collective-permute-start | bytes 1966088 | tf_op jit(solution)/shard_map/ppermute | solution.py:12
  345.8 30.8 %all-to-all-start.7 = ((bf16[8,2,128,512]{3,2,1,0:T(8,128)(2,1)}), bf16[8,2,128,512]{3,2,1,0:T(8,128)(2,1)S(1)}, u32[]{:S(2)}, u32[]{:S(2)}) async-start(bf16[8,2,128,512]{3,2,1,0:T(8,128)(2,1)} %copy.147), calls=%async_computation.7 | async-start | bytes 4194304 | tf_op jit(solution)/shard_map/all_to_all | solution.py:78
  382.7 20.4 %collective-permute-start.16 = (bf16[1280,2,128]{2,1,0:T(2,128)(2,1)}, bf16[1280,2,128]{2,1,0:T(2,128)(2,1)}, u32[]{:S(2)}, u32[]{:S(2)}) collective-permute-start(bf16[1280,2,128]{2,1,0:T(2,128)(2,1)} %fusion.86), channel_id=1, source_target_pairs={{0,2},{1,3},{2,4},{3,5},{4,6},{5,7},{6,8},{7,9},{8,10},{9,11},{10,... | collective-permute-start | bytes 1966088 | tf_op jit(solution)/shard_map/ppermute | solution.py:12
  382.7 50.0 %collective-permute-start.17 = (bf16[1280,2,128]{2,1,0:T(2,128)(2,1)}, bf16[1280,2,128]{2,1,0:T(2,128)(2,1)}, u32[]{:S(2)}, u32[]{:S(2)}) collective-permute-start(bf16[1280,2,128]{2,1,0:T(2,128)(2,1)} %fusion.87), channel_id=1, source_target_pairs={{0,3},{1,4},{2,5},{3,6},{4,7},{5,8},{6,9},{7,10},{8,11},{9,12},{10... | collective-permute-start | bytes 1966088 | tf_op jit(solution)/shard_map/ppermute | solution.py:12
  384.9 60.4 %collective-permute-start.9 = (bf16[1280,2,128]{2,1,0:T(2,128)(2,1)}, bf16[1280,2,128]{2,1,0:T(2,128)(2,1)}, u32[]{:S(2)}, u32[]{:S(2)}) collective-permute-start(bf16[1280,2,128]{2,1,0:T(2,128)(2,1)} %fusion.81), channel_id=1, source_target_pairs={{0,1},{1,2},{2,3},{3,4},{4,5},{5,6},{6,7},{7,8},{8,9},{9,10},{10,1... | collective-permute-start | bytes 1966088 | tf_op jit(solution)/shard_map/ppermute | solution.py:12
  388.6 68.5 %collective-permute-start.10 = (bf16[1280,2,128]{2,1,0:T(2,128)(2,1)}, bf16[1280,2,128]{2,1,0:T(2,128)(2,1)}, u32[]{:S(2)}, u32[]{:S(2)}) collective-permute-start(bf16[1280,2,128]{2,1,0:T(2,128)(2,1)} %fusion.82), channel_id=1, source_target_pairs={{0,2},{1,3},{2,4},{3,5},{4,6},{5,7},{6,8},{7,9},{8,10},{9,11},{10,... | collective-permute-start | bytes 1966088 | tf_op jit(solution)/shard_map/ppermute | solution.py:12
  391.4 88.2 %collective-permute-start.11 = (bf16[1280,2,128]{2,1,0:T(2,128)(2,1)S(1)}, bf16[1280,2,128]{2,1,0:T(2,128)(2,1)}, u32[]{:S(2)}, u32[]{:S(2)}) collective-permute-start(bf16[1280,2,128]{2,1,0:T(2,128)(2,1)S(1)} %fusion.83), channel_id=1, source_target_pairs={{0,3},{1,4},{2,5},{3,6},{4,7},{5,8},{6,9},{7,10},{8,11},{9,12},{10... | collective-permute-start | bytes 1966088 | tf_op jit(solution)/shard_map/ppermute | solution.py:12
  403.0 88.0 %collective-permute-start.21 = (bf16[1280,2,128]{2,1,0:T(2,128)(2,1)}, bf16[1280,2,128]{2,1,0:T(2,128)(2,1)}, u32[]{:S(2)}, u32[]{:S(2)}) collective-permute-start(bf16[1280,2,128]{2,1,0:T(2,128)(2,1)} %fusion.89), channel_id=1, source_target_pairs={{0,1},{1,2},{2,3},{3,4},{4,5},{5,6},{6,7},{7,8},{8,9},{9,10},{10,1... | collective-permute-start | bytes 1966088 | tf_op jit(solution)/shard_map/ppermute | solution.py:12
  432.7 58.3 %collective-permute-start.22 = (bf16[1280,2,128]{2,1,0:T(2,128)(2,1)}, bf16[1280,2,128]{2,1,0:T(2,128)(2,1)}, u32[]{:S(2)}, u32[]{:S(2)}) collective-permute-start(bf16[1280,2,128]{2,1,0:T(2,128)(2,1)} %fusion.90), channel_id=1, source_target_pairs={{0,2},{1,3},{2,4},{3,5},{4,6},{5,7},{6,8},{7,9},{8,10},{9,11},{10,... | collective-permute-start | bytes 1966088 | tf_op jit(solution)/shard_map/ppermute | solution.py:12
  445.3 61.8 %collective-permute-start.23 = (bf16[1280,2,128]{2,1,0:T(2,128)(2,1)}, bf16[1280,2,128]{2,1,0:T(2,128)(2,1)}, u32[]{:S(2)}, u32[]{:S(2)}) collective-permute-start(bf16[1280,2,128]{2,1,0:T(2,128)(2,1)} %fusion.91), channel_id=1, source_target_pairs={{0,3},{1,4},{2,5},{3,6},{4,7},{5,8},{6,9},{7,10},{8,11},{9,12},{10... | collective-permute-start | bytes 1966088 | tf_op jit(solution)/shard_map/ppermute | solution.py:12
  (20 other events, 318.1 us)
where the time goes:
time: 588 us; the launch traced here: 582 us
  blocking collectives  153 us (26%)
  waiting for transfers between devices  149 us (25%)
  matrix products  86.4 us (15%)
  local copies, waits for them, and re-layouts  82.5 us (14%)
  starting transfers between devices  72.9 us (12%)
  other arithmetic  36.3 us (6%)
    ppermute x24, waiting for transfers between devices, shifted(): lax.ppermute(array, axis, [(i, (i + by) % peers) for i in range(peers)])  81.1 us
    all_gather x4, blocking collectives, per_device(): lax.all_gather(lower_panel[front_index], 'pcol', axis=0, tiled=True)  78.2 us
    psum x1, blocking collectives, per_device(): solved = lax.psum(partial_panel, 'prow')  74.9 us
    all_to_all x4, waiting for transfers between devices, per_device(): lax.all_to_all(outgoing, 'prow', split_axis=0, concat_axis=0, tiled=True)  63.7 us
    dot_general x4, local copies, waits for them, and re-layouts, per_device(): jnp.einsum('qs,suv->quv', row_place, addition, preferred_element_type=jnp...  32.7 us
    ppermute x24, starting transfers between devices, shifted(): lax.ppermute(array, axis, [(i, (i + by) % peers) for i in range(peers)])  31.5 us
    dot_general x16, matrix products, pack_columns(): jnp.einsum('rkv,ck->rcv', pieces, select.astype(jnp.bfloat16), preferred_...  28.8 us
    dot_general x4, matrix products, per_device(): jnp.einsum('rsv,sq->rqv', gathered, column_place, preferred_element_type=...  24.5 us
  transfers between devices with their start and end apart: 32, of which 11 were waited for; matrix products, arithmetic and copies ran while one was open for 22% of the time, Pallas kernels for 0%

commit v1 on v0

v1 whole, which is shorter than its diff:
```python
import jax
import jax.numpy as jnp
from jax import lax
from jax.experimental import pallas as pl
from jax.experimental.pallas import tpu as pltpu
from jax.sharding import PartitionSpec as P

MESH = pl.DeviceIdType.MESH
TILE = 128
FRONTS = 4
NR = 8
NC = 16
REACH = 4
ROWS = 10
OWN_R = 16
OWN_C = 8
WIDTH = 512
EMPTY = REACH * 2 * ROWS
CUT = (0, 4, 10)
LAST = 2 * FRONTS - 1
DEPTH = 256
LP = 16
UP = 32


def wrap(value, n):
    return lax.rem(value + n, n)


def kernel(
    maps_s, maps_v, small, lower, update, parent, out,
    upd0, upd1, upd2, upd3, xr0, xr1, xr2, xr3, xr4, xr5, xr6, xr7, yr0, yr1, yr2, yr3,
    low, xs, ls, lr, low_all, s_all, sol, comp, ys, relay, acc,
    mapv, tabv, map_s, tab_s, rtab_s,
    m_ss, m_rs, l_ss, l_rs, s_ss, s_rs, x_ss, x_rs, g_ss, g_rs, z_ss, z_rs,
    y_ss, y_rs, q_ss, q_rs, loc, o_sem,
):
    upd, yr = (upd0, upd1, upd2, upd3), (yr0, yr1, yr2, yr3)
    xr = (xr0, xr1, xr2, xr3, xr4, xr5, xr6, xr7)
    r = lax.axis_index("prow")
    c = lax.axis_index("pcol")
    x = lax.div(r, 2)
    core = lax.rem(r, 2)
    z = lax.div(c, 4)
    y = lax.rem(c, 4)

    def row_to(i):
        return (lax.rem(x + i // 2, 4) * 2 + lax.rem(core + i % 2, 2), c)

    def col_to(e):
        return (r, lax.rem(c + e, NC))

    def remote(src, dst, ss, rs, to):
        return pltpu.make_async_remote_copy(
            src_ref=src, dst_ref=dst, send_sem=ss, recv_sem=rs, device_id=to, device_id_type=MESH
        )

    def start(copies):
        for cp in copies:
            cp.start()

    def wait_recv(copies):
        for cp in copies:
            cp.wait_recv()

    barrier = pltpu.get_barrier_semaphore()
    for i in range(1, NR):
        pl.semaphore_signal(barrier, inc=1, device_id=row_to(i), device_id_type=MESH)
    for e in range(1, NC):
        pl.semaphore_signal(barrier, inc=1, device_id=col_to(e), device_id_type=MESH)

    upd_cp = [pltpu.make_async_copy(update.at[f], upd[f], loc.at[f]) for f in range(FRONTS)]
    start(upd_cp)
    acc_cp = pltpu.make_async_copy(parent, acc, loc.at[4])
    acc_cp.start()

    lane = lax.broadcasted_iota(jnp.int32, (8, 128), 1)
    sub = lax.broadcasted_iota(jnp.int32, (8, 128), 0)
    first = jnp.full((8, 128), -1, jnp.int32)
    second = jnp.full((8, 128), -1, jnp.int32)
    for f in range(FRONTS):
        for k in range(12):
            m = maps_s[f, k]
            if k < 8:
                d = lax.div(m, OWN_R)
                at = wrap(lax.div(d, 2) - x, 4) * 2 + lax.rem(lax.rem(d, 2) + core, 2)
            else:
                at = 16 + wrap(lax.div(m, OWN_C) - c, NC)
            hit = (lane == at) & (sub == f)
            fresh = first < 0
            second = jnp.where(hit & jnp.logical_not(fresh), k % 8, second)
            first = jnp.where(hit & fresh, k % 8, first)
    tabv[0:8] = jnp.maximum(first, 0)
    tabv[8:16] = jnp.maximum(second, 0)
    t_cp = pltpu.make_async_copy(tabv.at[pl.ds(0, 16)], tab_s, loc.at[5])
    t_cp.start()
    t_cp.wait()

    for f in range(FRONTS):
        for k in range(8):
            low[f, k] = lower[f, :, k * TILE:(k + 1) * TILE]
        yr[f][EMPTY] = jnp.zeros((TILE, TILE), jnp.bfloat16)
    for i in range(NR):
        for f in range(FRONTS):
            for j in range(2):
                piece = low[f, tab_s[j * 8 + f, i]]
                if i:
                    ls[i - 1, f, j] = piece
                else:
                    lr[0, f, j] = piece
    mapv[0] = maps_v[...]
    s_all[pl.ds(r, 1)] = small[...][None]

    def pack_x(f):
        upd_cp[f].wait()

        def one(i, carry):
            for j in range(2):
                xs[f, j, i] = upd[f][tab_s[j * 8 + f, i + 1]]
            return carry

        lax.fori_loop(0, NR - 1, one, 0)
        for j in range(2):
            xr[2 * f + j][0] = upd[f][tab_s[j * 8 + f, 0]]

    m_cp = [remote(maps_v, mapv.at[i], m_ss.at[i], m_rs.at[i], row_to(i)) for i in range(1, NR)]
    m_cp += [
        remote(maps_v, mapv.at[7 + o], m_ss.at[7 + o], m_rs.at[7 + o], col_to(o))
        for o in range(1, REACH)
    ]
    l_cp = [remote(ls.at[i - 1], lr.at[i], l_ss.at[i], l_rs.at[i], row_to(i)) for i in range(1, NR)]
    s_cp = [
        [
            remote(small.at[f], s_all.at[r, f], s_ss.at[f, i], s_rs.at[f, i], row_to(i))
            for i in range(1, NR)
        ]
        for f in range(FRONTS)
    ]
    x_cp = [
        [
            remote(xs.at[n // 2, n % 2, i - 1], xr[n].at[i], x_ss.at[n, i], x_rs.at[n, i], row_to(i))
            for i in range(1, NR)
        ]
        for n in range(2 * FRONTS)
    ]

    def side(e):
        return (r, z * 4 + lax.rem(y + e, 4))

    g_cp = [
        [
            remote(
                low_all.at[f, c], low_all.at[f, c], g_ss.at[f, e], g_rs.at[f, e],
                side(e) if f else col_to(e),
            )
            for e in range(1, 4 if f else NC)
        ]
        for f in range(FRONTS)
    ]

    def ring(f, s):
        block = low_all.at[f, pl.ds(lax.rem(z + s - 1, 4) * 4, 4)]
        return remote(block, block, z_ss.at[f, s], z_rs.at[f, s], col_to(NC - 4))

    z_cp = [[ring(f, s) for s in range(1, 4)] if f else [] for f in range(FRONTS)]

    def y_parts(n):
        f, h = n // 2, n % 2
        base, size = 2 * CUT[h], 2 * (CUT[h + 1] - CUT[h])
        return f, h, pl.ds(base, size), lambda o: pl.ds(o * 2 * ROWS + base, size)

    def y_copy(n, o):
        f, h, src, dst = y_parts(n)
        return remote(
            ys.at[f, o - 1, src], yr[f].at[dst(o)], y_ss.at[n, o], y_rs.at[n, o], col_to(o)
        )

    def relay_copy(n):
        f, h, src, _ = y_parts(n)
        return remote(
            ys.at[f, 0, src], relay.at[f, src], y_ss.at[n, 1], q_rs.at[n], col_to(4)
        )

    def forward_copy(n):
        f, h, src, dst = y_parts(n)
        return remote(
            relay.at[f, src], yr[f].at[dst(1)], q_ss.at[n], y_rs.at[n, 1], col_to(NC - 3)
        )

    edge = y == 3

    pack_x(0)
    pl.semaphore_wait(barrier, NR - 1 + NC - 1)
    start(m_cp)
    start(l_cp)
    start(s_cp[0])
    start(x_cp[0])

    wait_recv(m_cp)
    map_cp = pltpu.make_async_copy(mapv, map_s, loc.at[6])
    map_cp.start()
    map_cp.wait()

    for f in range(FRONTS):

        def count(i, total):
            held = jnp.int32(0)
            for k in range(8):
                held = held | jnp.where(lax.div(map_s[i, f, k], OWN_R) == r, 1, 0)
            return total + held

        heads = lax.fori_loop(0, NR, count, jnp.int32(0))

        def from_row(i, carry):
            table, q_first, q_second = carry
            rank = jnp.int32(0)
            for k in range(8):
                m = map_s[i, f, k]
                mine = lax.div(m, OWN_R) == r
                q = jnp.where(rank == 0, q_first, q_second)
                table = jnp.where(lane == jnp.where(mine, lax.rem(m, OWN_R), -1), q, table)
                table = jnp.where(lane == jnp.where(mine, 32 + q, -1), rank * 8 + i, table)
                q_first = q_first + jnp.where(mine & (rank == 0), 1, 0)
                q_second = q_second + jnp.where(mine & (rank > 0), 1, 0)
                rank = rank + jnp.where(mine, 1, 0)
            return table, q_first, q_second

        places, _, _ = lax.fori_loop(
            0, NR, from_row,
            (jnp.full((8, 128), -1, jnp.int32), jnp.int32(0), jnp.maximum(heads, CUT[1])),
        )
        for o in range(REACH):
            rank = jnp.int32(0)
            for k in range(4):
                m = map_s[0 if o == 0 else 7 + o, f, 8 + k]
                mine = lax.div(m, OWN_C) == c
                at_place = jnp.where(mine, 64 + lax.rem(m, OWN_C), -1)
                places = jnp.where(lane == at_place, o * 2 + rank, places)
                rank = rank + jnp.where(mine, 1, 0)
        tabv[16 + 8 * f:24 + 8 * f] = places
        r_cp = pltpu.make_async_copy(tabv.at[pl.ds(16 + 8 * f, 8)], rtab_s.at[f], loc.at[7])
        r_cp.start()
        r_cp.wait()

        if f == 0:
            wait_recv(l_cp)

        def take(q, carry):
            slot = jnp.clip(rtab_s[f, 0, 32 + q], 0, 15)
            low_all[f, c, q] = lr[lax.rem(slot, 8), f, lax.div(slot, 8)]
            return carry

        lax.fori_loop(0, ROWS, take, 0)
        start(g_cp[f])
        if f == 0:
            start(x_cp[1])

    pack_x(1)

    def out_copy(p):
        return pltpu.make_async_copy(acc.at[p], out.at[p], o_sem.at[p])

    def assemble(f):
        def one(p, carry):
            q = rtab_s[f, 0, p]
            late = q >= CUT[1]
            size = jnp.where(late, ROWS - CUT[1], CUT[1])
            base = jnp.where(late, CUT[1], 0) + jnp.minimum(q, ROWS - 1)
            for t in range(OWN_C):
                slot = rtab_s[f, 0, 64 + t]
                held = (q >= 0) & (slot >= 0)
                slot = jnp.minimum(slot, 2 * REACH - 1)
                at = lax.div(slot, 2) * (2 * ROWS) + lax.rem(slot, 2) * size + base
                tile = yr[f][jnp.where(held, at, EMPTY)]
                cols = pl.ds(t * TILE, TILE)
                acc[p, :, cols] = acc[p, :, cols] + tile.astype(jnp.float32)
            if f == FRONTS - 1:
                out_copy(p).start()
            return carry

        lax.fori_loop(0, OWN_R, one, 0)

    def y_wait(n):
        for o in range(1, REACH):
            y_copy(n, o).wait_recv()

    def pass_on(n):
        @pl.when(edge)
        def _():
            relay_copy(n).wait_recv()
            forward_copy(n).start()

    for n in range(2 * FRONTS):
        f, h = n // 2, n % 2
        low_q, high_q = CUT[h], CUT[h + 1]
        if h == 0:
            wait_recv(s_cp[f])
            left = s_all[:, f, :, 0:DEPTH].reshape(DEPTH, DEPTH)
            right = s_all[:, f, :, DEPTH:].reshape(DEPTH, WIDTH)
            sol[...] = lax.dot_general(
                left, right, (((0,), (0,)), ((), ())), preferred_element_type=jnp.float32
            ).astype(jnp.bfloat16)
            wait_recv(g_cp[0] if f == 0 else z_cp[f][2:])
        wait_recv(x_cp[n])
        if n + 2 <= LAST:
            if h == 0:
                start(s_cp[f + 1])
            start(x_cp[n + 2])
        if n:
            pass_on(n - 1)

        def subtract(q, carry):
            slot = jnp.clip(rtab_s[f, 0, 32 + q], 0, 15)
            i = lax.rem(slot, 8)
            piece = xr[2 * f][i].astype(jnp.float32)
            if h:
                piece = jnp.where(slot >= 8, xr[2 * f + 1][i].astype(jnp.float32), piece)
            product = lax.dot_general(
                low_all[f, :, q].reshape(DEPTH, TILE), sol[...],
                (((0,), (0,)), ((), ())), preferred_element_type=jnp.float32,
            )
            rest = (piece - product).astype(jnp.bfloat16)
            for k in range(4):
                comp[k, q] = rest[:, k * TILE:(k + 1) * TILE]
            return carry

        lax.fori_loop(low_q, high_q, subtract, 0)
        size = high_q - low_q
        for o in (1, 3, 2, 0):
            for j in range(2):
                k = jnp.minimum(tab_s[j * 8 + f, 16 + o], 3)
                at = 2 * low_q + j * size
                if o:
                    ys[f, o - 1, at:at + size] = comp[k, low_q:high_q]
                else:
                    yr[f][at:at + size] = comp[k, low_q:high_q]
            if o == 1:
                pl.when(edge)(lambda: relay_copy(n).start())
                pl.when(jnp.logical_not(edge))(lambda: y_copy(n, 1).start())
            elif o:
                y_copy(n, o).start()
        if f + 1 < FRONTS:
            if h == 0:
                wait_recv(g_cp[f + 1])
                z_cp[f + 1][0].start()
            else:
                z_cp[f + 1][0].wait_recv()
                z_cp[f + 1][1].start()
                if f + 2 < FRONTS:
                    pack_x(f + 2)
                z_cp[f + 1][1].wait_recv()
                z_cp[f + 1][2].start()
        if f >= 2 and h == 0:
            if f == 2:
                acc_cp.wait()
            y_wait(2 * f - 4)
            y_wait(2 * f - 3)
            assemble(f - 2)
    pass_on(LAST)
    for f in (FRONTS - 2, FRONTS - 1):
        y_wait(2 * f)
        y_wait(2 * f + 1)
        assemble(f)
    for cp in m_cp + l_cp + sum(s_cp + x_cp + g_cp + z_cp[1:], []):
        cp.wait_send()
    for n in range(2 * FRONTS):
        for o in range(1, REACH):
            y_copy(n, o).wait_send()
        pl.when(edge)(lambda: forward_copy(n).wait_send())
    for p in range(OWN_R):
        out_copy(p).wait()


def per_device(pivot_inverse, upper, lower, update, row_map, column_map, parent):
    small = jnp.concatenate([jnp.swapaxes(pivot_inverse, 1, 2), upper], axis=2)
    maps = jnp.pad(jnp.concatenate([row_map, column_map], axis=1), ((0, 4), (0, 116)))
    held = (OWN_R, TILE, OWN_C * TILE)
    dma = pltpu.SemaphoreType.DMA
    bf = jnp.bfloat16
    vmem = pl.BlockSpec(memory_space=pltpu.VMEM)
    anywhere = pl.BlockSpec(memory_space=pl.ANY)
    return pl.pallas_call(
        kernel,
        out_shape=jax.ShapeDtypeStruct(held, parent.dtype),
        in_specs=[pl.BlockSpec(memory_space=pltpu.SMEM), vmem, vmem, vmem, anywhere, anywhere],
        out_specs=anywhere,
        scratch_shapes=[
            *[pltpu.VMEM((8, TILE, WIDTH), bf)] * FRONTS,
            *[pltpu.VMEM((NR, TILE, WIDTH), bf)] * (2 * FRONTS),
            *[pltpu.VMEM((EMPTY + 1, TILE, TILE), bf)] * FRONTS,
            pltpu.VMEM((FRONTS, 8, LP, TILE), bf),
            pltpu.VMEM((FRONTS, 2, NR - 1, TILE, WIDTH), bf),
            pltpu.VMEM((NR - 1, FRONTS, 2, LP, TILE), bf),
            pltpu.VMEM((NR, FRONTS, 2, LP, TILE), bf),
            pltpu.VMEM((FRONTS, NC, ROWS, LP, TILE), bf),
            pltpu.VMEM((NR, FRONTS, UP, DEPTH + WIDTH), bf),
            pltpu.VMEM((DEPTH, WIDTH), bf),
            pltpu.VMEM((4, ROWS, TILE, TILE), bf),
            pltpu.VMEM((FRONTS, REACH - 1, 2 * ROWS, TILE, TILE), bf),
            pltpu.VMEM((FRONTS, 2 * ROWS, TILE, TILE), bf),
            pltpu.VMEM(held, parent.dtype),
            pltpu.VMEM((11, 8, 128), jnp.int32),
            pltpu.VMEM((48, 128), jnp.int32),
            pltpu.SMEM((11, 8, 128), jnp.int32),
            pltpu.SMEM((16, 128), jnp.int32),
            pltpu.SMEM((FRONTS, 8, 128), jnp.int32),
            dma((11,)), dma((11,)),
            dma((NR,)), dma((NR,)),
            dma((FRONTS, NR)), dma((FRONTS, NR)),
            dma((2 * FRONTS, NR)), dma((2 * FRONTS, NR)),
            dma((FRONTS, NC)), dma((FRONTS, NC)),
            dma((FRONTS, 4)), dma((FRONTS, 4)),
            dma((2 * FRONTS, REACH)), dma((2 * FRONTS, REACH)),
            dma((2 * FRONTS,)), dma((2 * FRONTS,)),
            dma((8,)),
            dma((OWN_R,)),
        ],
        compiler_params=pltpu.CompilerParams(
            collective_id=0, has_side_effects=True, vmem_limit_bytes=60 * 1024 * 1024
        ),
        name="fronts",
    )(
        maps, maps, small, lower,
        update.reshape(FRONTS, 8, TILE, WIDTH), parent.reshape(held),
    ).reshape(parent.shape)


def solution(mesh):
    in_specs = (
        P(None, None, "prow"),
        P(None, "prow", "pcol"),
        P(None, "pcol", "prow"),
        P(None, "prow", "pcol"),
        P(None, "prow"),
        P(None, "pcol"),
        P("prow", "pcol"),
    )
    return jax.shard_map(
        per_device, mesh=mesh, in_specs=in_specs, out_specs=P("prow", "pcol"), check_vma=False
    )
```

time: 588 us -> 174 us (0.30); the launches traced: 582 us -> 174 us
  Pallas kernels: 0 us -> 163 us
  blocking collectives: 153 us -> 0 us
  waiting for transfers between devices: 149 us -> 0 us
  matrix products: 86.4 us -> 0 us
  local copies, waits for them, and re-layouts: 82.5 us -> 9.04 us
  starting transfers between devices: 72.9 us -> 0 us
  other arithmetic: 36.3 us -> 2.37 us
    pallas_call x0 -> x1, Pallas kernels: none -> 163 us  [per_device(): pl.pallas_call(kernel, out_shape=jax.ShapeDtypeStruct(held, parent.dtype)...]
    dot_general x40 -> x0, matrix products: 86.4 us -> none  [the longest x16 28.8 us: pack_columns(): jnp.einsum('rkv,ck->rcv', pieces, select.astype(jnp.bfloat16), preferred_...]
    ppermute x24 -> x0, waiting for transfers between devices: 81.1 us -> none  [shifted(): lax.ppermute(array, axis, [(i, (i + by) % peers) for i in range(peers)])]
    all_gather x4 -> x0, blocking collectives: 78.2 us -> none  [per_device(): lax.all_gather(lower_panel[front_index], 'pcol', axis=0, tiled=True)]
    psum x1 -> x0, blocking collectives: 74.9 us -> none  [per_device(): solved = lax.psum(partial_panel, 'prow')]
    all_to_all x8 -> x0, waiting for transfers between devices: 68.4 us -> none  [the longest x4 63.7 us: per_device(): lax.all_to_all(outgoing, 'prow', split_axis=0, concat_axis=0, tiled=True)]
    all_to_all x8 -> x0, starting transfers between devices: 41.4 us -> none  [the longest x4 22.6 us: per_device(): lax.all_to_all(tile_label, 'prow', split_axis=0, concat_axis=0, tiled=True)]
    dot_general x4 -> x0, local copies, waits for them, and re-layouts: 32.7 us -> none  [per_device(): jnp.einsum('qs,suv->quv', row_place, addition, preferred_element_type=jnp...]
  transfers between devices with their start and end apart: 32 -> 0, of which waited for: 11 -> 0; matrix products, arithmetic and copies ran while one was open for 22% -> 0% of each run, Pallas kernels for 0% -> 0%
where the time goes in v1:
time: 174 us
  Pallas kernels  163 us (94%)
  local copies, waits for them, and re-layouts  9.04 us (5%)
  other arithmetic  2.37 us (1%)
    pallas_call x1, Pallas kernels, per_device(): pl.pallas_call(kernel, out_shape=jax.ShapeDtypeStruct(held, parent.dtype)...  163 us
    unnamed x1, local copies, waits for them, and re-layouts  8.44 us

profile of v1, /device:TPU:1, one launch (start us, length us, event | category | flops | bytes accessed | tf_op | source)
XLA Modules:
  0.0 174.1 jit_solution(1593657578981650822)
XLA Ops:
  0.0 0.8 pad_add_fusion
  0.8 0.6 pad.4.maps_s.maps_v
  1.4 1.6 pad_maximum_fusion.small
  3.0 162.7 %fronts.1 = f32[16,128,1024]{2,1,0:T(8,128)} custom-call(s32[8,128]{1,0:T(8,128)} %pad.4.maps_s.maps_v, s32[8,128]{1,0:T(8,128)} %pad.4.maps_s.maps_v, bf16[4,32,768]{2,1,0:T(8,128)(2,1)} %pad_maximum_fusion.small, bf16[4,16,1024]{2,1,0:T(8,128)(2,1)} %lower.1, bf16[4,8,128,512]{3,2,1,0:T(8,128)(2,1)} %bitcast.6, f32[16,128,1024]{2,1,0:T(8,128)} %bitcast.5), custom_call_target="tpu_custom_call" | custom-call | tf_op jit(solution)/shard_map/fronts/pallas_call | solution.py:382
  165.7 8.4 %copy.9 = f32[2048,1024]{1,0:T(8,128)} copy(f32[2048,1024]{1,0:T(8,128)} %bitcast.4) | data formatting | bytes 16777216

commit v2 on v1

--- a/solution.py
+++ b/solution.py
@@ -28,14 +28,14 @@
 
 
 def kernel(
-    maps_s, maps_v, small, lower, update, parent, out,
-    upd0, upd1, upd2, upd3, xr0, xr1, xr2, xr3, xr4, xr5, xr6, xr7, yr0, yr1, yr2, yr3,
-    low, xs, ls, lr, low_all, s_all, sol, comp, ys, relay, acc,
+    rows_s, cols_s, pivot, upper, lower, update, parent, early, last, last_tab,
+    upd0, upd1, upd2, upd3, xr0, xr1, xr2, xr3, xr4, xr5, xr6, xr7, yr0, yr1, yr2,
+    low, xs, ls, lr, low_all, s_all, sol, comp, ys, own, relay, acc,
     mapv, tabv, map_s, tab_s, rtab_s,
     m_ss, m_rs, l_ss, l_rs, s_ss, s_rs, x_ss, x_rs, g_ss, g_rs, z_ss, z_rs,
-    y_ss, y_rs, q_ss, q_rs, loc, o_sem,
+    y_ss, y_rs, q_ss, q_rs, loc, own_sem, o_sem,
 ):
-    upd, yr = (upd0, upd1, upd2, upd3), (yr0, yr1, yr2, yr3)
+    upd, yr = (upd0, upd1, upd2, upd3), (yr0, yr1, yr2, last)
     xr = (xr0, xr1, xr2, xr3, xr4, xr5, xr6, xr7)
     r = lax.axis_index("prow")
     c = lax.axis_index("pcol")
@@ -78,9 +78,11 @@
     sub = lax.broadcasted_iota(jnp.int32, (8, 128), 0)
     first = jnp.full((8, 128), -1, jnp.int32)
     second = jnp.full((8, 128), -1, jnp.int32)
+    tile_map = jnp.zeros((8, 128), jnp.int32)
     for f in range(FRONTS):
         for k in range(12):
-            m = maps_s[f, k]
+            m = rows_s[f, k] if k < 8 else cols_s[f, k - 8]
+            tile_map = jnp.where((lane == k) & (sub == f), m, tile_map)
             if k < 8:
                 d = lax.div(m, OWN_R)
                 at = wrap(lax.div(d, 2) - x, 4) * 2 + lax.rem(lax.rem(d, 2) + core, 2)
@@ -94,22 +96,10 @@
     tabv[8:16] = jnp.maximum(second, 0)
     t_cp = pltpu.make_async_copy(tabv.at[pl.ds(0, 16)], tab_s, loc.at[5])
     t_cp.start()
-    t_cp.wait()
-
+    mapv[0] = tile_map
     for f in range(FRONTS):
-        for k in range(8):
-            low[f, k] = lower[f, :, k * TILE:(k + 1) * TILE]
-        yr[f][EMPTY] = jnp.zeros((TILE, TILE), jnp.bfloat16)
-    for i in range(NR):
-        for f in range(FRONTS):
-            for j in range(2):
-                piece = low[f, tab_s[j * 8 + f, i]]
-                if i:
-                    ls[i - 1, f, j] = piece
-                else:
-                    lr[0, f, j] = piece
-    mapv[0] = maps_v[...]
-    s_all[pl.ds(r, 1)] = small[...][None]
+        s_all[r, f, :, 0:DEPTH] = pivot[f]
+        s_all[r, f, :, DEPTH:] = upper[f]
 
     def pack_x(f):
         upd_cp[f].wait()
@@ -123,15 +113,15 @@
         for j in range(2):
             xr[2 * f + j][0] = upd[f][tab_s[j * 8 + f, 0]]
 
-    m_cp = [remote(maps_v, mapv.at[i], m_ss.at[i], m_rs.at[i], row_to(i)) for i in range(1, NR)]
+    m_cp = [remote(mapv.at[0], mapv.at[i], m_ss.at[i], m_rs.at[i], row_to(i)) for i in range(1, NR)]
     m_cp += [
-        remote(maps_v, mapv.at[7 + o], m_ss.at[7 + o], m_rs.at[7 + o], col_to(o))
+        remote(mapv.at[0], mapv.at[7 + o], m_ss.at[7 + o], m_rs.at[7 + o], col_to(o))
         for o in range(1, REACH)
     ]
     l_cp = [remote(ls.at[i - 1], lr.at[i], l_ss.at[i], l_rs.at[i], row_to(i)) for i in range(1, NR)]
     s_cp = [
         [
-            remote(small.at[f], s_all.at[r, f], s_ss.at[f, i], s_rs.at[f, i], row_to(i))
+            remote(s_all.at[r, f], s_all.at[r, f], s_ss.at[f, i], s_rs.at[f, i], row_to(i))
             for i in range(1, NR)
         ]
         for f in range(FRONTS)
@@ -187,14 +177,32 @@
             relay.at[f, src], yr[f].at[dst(1)], q_ss.at[n], y_rs.at[n, 1], col_to(NC - 3)
         )
 
+    def own_copy(n):
+        f, h, src, _ = y_parts(n)
+        return pltpu.make_async_copy(own.at[src], last.at[src], own_sem.at[h])
+
     edge = y == 3
 
-    pack_x(0)
     pl.semaphore_wait(barrier, NR - 1 + NC - 1)
     start(m_cp)
+    t_cp.wait()
+    for f in range(FRONTS):
+        for k in range(8):
+            low[f, k] = lower[f, :, k * TILE:(k + 1) * TILE]
+    for i in range(NR):
+        for f in range(FRONTS):
+            for j in range(2):
+                piece = low[f, tab_s[j * 8 + f, i]]
+                if i:
+                    ls[i - 1, f, j] = piece
+                else:
+                    lr[0, f, j] = piece
     start(l_cp)
     start(s_cp[0])
+    pack_x(0)
     start(x_cp[0])
+    for f in range(FRONTS - 1):
+        yr[f][EMPTY] = jnp.zeros((TILE, TILE), jnp.bfloat16)
 
     wait_recv(m_cp)
     map_cp = pltpu.make_async_copy(mapv, map_s, loc.at[6])
@@ -251,14 +259,14 @@
             return carry
 
         lax.fori_loop(0, ROWS, take, 0)
-        start(g_cp[f])
         if f == 0:
-            start(x_cp[1])
-
-    pack_x(1)
+            start(g_cp[0])
+            pack_x(1)
+    last_tab[...] = places
+    start(x_cp[1])
 
     def out_copy(p):
-        return pltpu.make_async_copy(acc.at[p], out.at[p], o_sem.at[p])
+        return pltpu.make_async_copy(acc.at[p], early.at[p], o_sem.at[p])
 
     def assemble(f):
         def one(p, carry):
@@ -274,7 +282,7 @@
                 tile = yr[f][jnp.where(held, at, EMPTY)]
                 cols = pl.ds(t * TILE, TILE)
                 acc[p, :, cols] = acc[p, :, cols] + tile.astype(jnp.float32)
-            if f == FRONTS - 1:
+            if f == FRONTS - 2:
                 out_copy(p).start()
             return carry
 
@@ -308,6 +316,8 @@
             start(x_cp[n + 2])
         if n:
             pass_on(n - 1)
+        if h == 0 and f + 1 < FRONTS:
+            start(g_cp[f + 1])
 
         def subtract(q, carry):
             slot = jnp.clip(rtab_s[f, 0, 32 + q], 0, 15)
@@ -332,6 +342,8 @@
                 at = 2 * low_q + j * size
                 if o:
                     ys[f, o - 1, at:at + size] = comp[k, low_q:high_q]
+                elif f == FRONTS - 1:
+                    own[at:at + size] = comp[k, low_q:high_q]
                 else:
                     yr[f][at:at + size] = comp[k, low_q:high_q]
             if o == 1:
@@ -339,6 +351,8 @@
                 pl.when(jnp.logical_not(edge))(lambda: y_copy(n, 1).start())
             elif o:
                 y_copy(n, o).start()
+            elif f == FRONTS - 1:
+                own_copy(n).start()
         if f + 1 < FRONTS:
             if h == 0:
                 wait_recv(g_cp[f + 1])
@@ -357,10 +371,13 @@
             y_wait(2 * f - 3)
             assemble(f - 2)
     pass_on(LAST)
-    for f in (FRONTS - 2, FRONTS - 1):
-        y_wait(2 * f)
-        y_wait(2 * f + 1)
-        assemble(f)
+    y_wait(LAST - 3)
+    y_wait(LAST - 2)
+    assemble(FRONTS - 2)
+    y_wait(LAST - 1)
+    y_wait(LAST)
+    own_copy(LAST - 1).wait()
+    own_copy(LAST).wait()
     for cp in m_cp + l_cp + sum(s_cp + x_cp + g_cp + z_cp[1:], []):
         cp.wait_send()
     for n in range(2 * FRONTS):
@@ -371,23 +388,77 @@
         out_copy(p).wait()
 
 
+def finish(tab, early, last, out, held, tiles, a_sem, t_sem, o_sem):
+    def read(p):
+        return pltpu.make_async_copy(early.at[p], held.at[p], a_sem.at[p])
+
+    def write(p):
+        return pltpu.make_async_copy(held.at[p], out.at[p], o_sem.at[p])
+
+    def reads(p, carry):
+        read(p).start()
+        return carry
+
+    tiles_cp = pltpu.make_async_copy(last, tiles, t_sem)
+    tiles_cp.start()
+    lax.fori_loop(0, OWN_R, reads, 0)
+    tiles_cp.wait()
+
+    def one(p, carry):
+        q = tab[0, p]
+
+        @pl.when(p >= 0)
+        def _():
+            read(p).wait()
+
+            @pl.when(q >= 0)
+            def _():
+                late = q >= CUT[1]
+                size = jnp.where(late, ROWS - CUT[1], CUT[1])
+                base = jnp.where(late, CUT[1], 0) + jnp.minimum(q, ROWS - 1)
+                for t in range(OWN_C):
+                    slot = tab[0, 64 + t]
+
+                    @pl.when(slot >= 0)
+                    def _():
+                        place = jnp.minimum(slot, 2 * REACH - 1)
+                        at = lax.div(place, 2) * (2 * ROWS) + lax.rem(place, 2) * size + base
+                        cols = pl.ds(t * TILE, TILE)
+                        held[p, :, cols] = held[p, :, cols] + tiles[at].astype(jnp.float32)
+
+            write(p).start()
+
+        return carry
+
+    lax.fori_loop(0, OWN_R, one, 0)
+
+    def ends(p, carry):
+        write(p).wait()
+        return carry
+
+    lax.fori_loop(0, OWN_R, ends, 0)
+
+
 def per_device(pivot_inverse, upper, lower, update, row_map, column_map, parent):
-    small = jnp.concatenate([jnp.swapaxes(pivot_inverse, 1, 2), upper], axis=2)
-    maps = jnp.pad(jnp.concatenate([row_map, column_map], axis=1), ((0, 4), (0, 116)))
     held = (OWN_R, TILE, OWN_C * TILE)
     dma = pltpu.SemaphoreType.DMA
     bf = jnp.bfloat16
     vmem = pl.BlockSpec(memory_space=pltpu.VMEM)
     anywhere = pl.BlockSpec(memory_space=pl.ANY)
-    return pl.pallas_call(
+    scalars = pl.BlockSpec(memory_space=pltpu.SMEM)
+    early, last, table = pl.pallas_call(
         kernel,
-        out_shape=jax.ShapeDtypeStruct(held, parent.dtype),
-        in_specs=[pl.BlockSpec(memory_space=pltpu.SMEM), vmem, vmem, vmem, anywhere, anywhere],
-        out_specs=anywhere,
+        out_shape=(
+            jax.ShapeDtypeStruct(held, parent.dtype),
+            jax.ShapeDtypeStruct((EMPTY, TILE, TILE), bf),
+            jax.ShapeDtypeStruct((8, 128), jnp.int32),
+        ),
+        in_specs=[scalars, scalars, vmem, vmem, vmem, anywhere, anywhere],
+        out_specs=(anywhere, anywhere, vmem),
         scratch_shapes=[
             *[pltpu.VMEM((8, TILE, WIDTH), bf)] * FRONTS,
             *[pltpu.VMEM((NR, TILE, WIDTH), bf)] * (2 * FRONTS),
-            *[pltpu.VMEM((EMPTY + 1, TILE, TILE), bf)] * FRONTS,
+            *[pltpu.VMEM((EMPTY + 1, TILE, TILE), bf)] * (FRONTS - 1),
             pltpu.VMEM((FRONTS, 8, LP, TILE), bf),
             pltpu.VMEM((FRONTS, 2, NR - 1, TILE, WIDTH), bf),
             pltpu.VMEM((NR - 1, FRONTS, 2, LP, TILE), bf),
@@ -397,6 +468,7 @@
             pltpu.VMEM((DEPTH, WIDTH), bf),
             pltpu.VMEM((4, ROWS, TILE, TILE), bf),
             pltpu.VMEM((FRONTS, REACH - 1, 2 * ROWS, TILE, TILE), bf),
+            pltpu.VMEM((2 * ROWS, TILE, TILE), bf),
             pltpu.VMEM((FRONTS, 2 * ROWS, TILE, TILE), bf),
             pltpu.VMEM(held, parent.dtype),
             pltpu.VMEM((11, 8, 128), jnp.int32),
@@ -413,6 +485,7 @@
             dma((2 * FRONTS, REACH)), dma((2 * FRONTS, REACH)),
             dma((2 * FRONTS,)), dma((2 * FRONTS,)),
             dma((8,)),
+            dma((2,)),
             dma((OWN_R,)),
         ],
         compiler_params=pltpu.CompilerParams(
@@ -420,9 +493,24 @@
         ),
         name="fronts",
     )(
-        maps, maps, small, lower,
+        row_map, column_map, jnp.swapaxes(pivot_inverse, 1, 2), upper, lower,
         update.reshape(FRONTS, 8, TILE, WIDTH), parent.reshape(held),
-    ).reshape(parent.shape)
+    )
+    return pl.pallas_call(
+        finish,
+        out_shape=jax.ShapeDtypeStruct(held, parent.dtype),
+        in_specs=[scalars, anywhere, anywhere],
+        out_specs=anywhere,
+        scratch_shapes=[
+            pltpu.VMEM(held, parent.dtype),
+            pltpu.VMEM((EMPTY, TILE, TILE), bf),
+            dma((OWN_R,)),
+            dma,
+            dma((OWN_R,)),
+        ],
+        compiler_params=pltpu.CompilerParams(vmem_limit_bytes=60 * 1024 * 1024),
+        name="finish",
+    )(table, early, last).reshape(parent.shape)
 
 
 def solution(mesh):

time: 174 us -> 172 us (0.989)
  local copies, waits for them, and re-layouts: 9.04 us -> 0 us
  Pallas kernels: 163 us -> 172 us
  other arithmetic: 2.37 us -> 0 us
    pallas_call x1 -> x2, Pallas kernels: 163 us -> 172 us  [the longest x1 164 us: per_device(): pl.pallas_call(kernel, out_shape=(jax.ShapeDtypeStruct(held, parent.dtype...]
    unnamed x1 -> x0, local copies, waits for them, and re-layouts: 8.44 us -> none
    concatenate x2 -> x0, other arithmetic: 2.37 us -> none  [the longest x1 1.6 us: per_device(): small = jnp.concatenate([jnp.swapaxes(pivot_inverse, 1, 2), upper], axis=2)]
where the time goes in v2:
time: 172 us
  Pallas kernels  172 us (100%)
    pallas_call x1, Pallas kernels, per_device(): pl.pallas_call(kernel, out_shape=(jax.ShapeDtypeStruct(held, parent.dtype...  164 us
    pallas_call x1, Pallas kernels, per_device(): pl.pallas_call(finish, out_shape=jax.ShapeDtypeStruct(held, parent.dtype)...  7.97 us

profile of v2, /device:TPU:1, one launch (start us, length us, event | category | flops | bytes accessed | tf_op | source)
XLA Modules:
  0.0 172.0 jit_solution(4476030761895524890)
XLA Ops:
  0.0 164.0 %fronts.1 = (f32[16,128,1024]{2,1,0:T(8,128)}, bf16[80,128,128]{2,1,0:T(8,128)(2,1)}, s32[8,128]{1,0:T(8,128)}) custom-call(s32[4,8]{1,0:T(4,128)} %rows_s.1, s32[4,4]{1,0:T(4,128)} %cols_s.1, bf16[4,32,256]{2,1,0:T(8,128)(2,1)} %bitcast.6, bf16[4,32,512]{2,1,0:T(8,128)(2,1)} %upper.1, bf16[4,16,1024]{2,1,0:T(8,128)(2,1)} %lower.1, ...), custom_call_target="tpu_custom_call" | custom-call | tf_op jit(solution)/shard_map/fronts/pallas_call | solution.py:449
  164.0 8.0 %finish.1 = f32[16,128,1024]{2,1,0:T(8,128)} custom-call(s32[8,128]{1,0:T(8,128)} %get-tuple-element.8.tab, f32[16,128,1024]{2,1,0:T(8,128)} %get-tuple-element.9.early, bf16[80,128,128]{2,1,0:T(8,128)(2,1)} %get-tuple-element.10.last), custom_call_target="tpu_custom_call" | custom-call | tf_op jit(solution)/shard_map/finish/pallas_call | solution.py:499

commit v3 on v2

--- a/solution.py
+++ b/solution.py
@@ -17,7 +17,8 @@
 WIDTH = 512
 EMPTY = REACH * 2 * ROWS
 CUT = (0, 4, 10)
-LAST = 2 * FRONTS - 1
+EARLY = FRONTS - 1
+CHUNKS = 2 * EARLY
 DEPTH = 256
 LP = 16
 UP = 32
@@ -29,14 +30,15 @@
 
 def kernel(
     rows_s, cols_s, pivot, upper, lower, update, parent, early, last, last_tab,
-    upd0, upd1, upd2, upd3, xr0, xr1, xr2, xr3, xr4, xr5, xr6, xr7, yr0, yr1, yr2,
-    low, xs, ls, lr, low_all, s_all, sol, comp, ys, own, relay, acc,
+    upd0, upd1, upd2, upd3, xr0, xr1, xr2, xr3, xr4, xr5, yr0, yr1, yr2,
+    low, xs, ls, lr, low_all, low_wide, s_all, sol, comp, ys, relay,
+    ys_wide, yr_wide, relay_wide, xs_wide, own, acc,
     mapv, tabv, map_s, tab_s, rtab_s,
     m_ss, m_rs, l_ss, l_rs, s_ss, s_rs, x_ss, x_rs, g_ss, g_rs, z_ss, z_rs,
     y_ss, y_rs, q_ss, q_rs, loc, own_sem, o_sem,
 ):
-    upd, yr = (upd0, upd1, upd2, upd3), (yr0, yr1, yr2, last)
-    xr = (xr0, xr1, xr2, xr3, xr4, xr5, xr6, xr7)
+    upd, yr = (upd0, upd1, upd2, upd3), (yr0, yr1, yr2)
+    xr = (xr0, xr1, xr2, xr3, xr4, xr5)
     r = lax.axis_index("prow")
     c = lax.axis_index("pcol")
     x = lax.div(r, 2)
@@ -119,19 +121,46 @@
         for o in range(1, REACH)
     ]
     l_cp = [remote(ls.at[i - 1], lr.at[i], l_ss.at[i], l_rs.at[i], row_to(i)) for i in range(1, NR)]
-    s_cp = [
-        [
-            remote(s_all.at[r, f], s_all.at[r, f], s_ss.at[f, i], s_rs.at[f, i], row_to(i))
-            for i in range(1, NR)
-        ]
-        for f in range(FRONTS)
-    ]
+    def s_copy(f, i):
+        slot = r if i % 2 == 0 or i == 1 else lax.rem(x - i // 2 + 4, 4) * 2 + core
+        block = s_all.at[slot, f]
+        to = i if i % 2 == 0 else 1
+        return remote(block, block, s_ss.at[f, i], s_rs.at[f, i], row_to(to))
+
+    s_cp = [[s_copy(f, i) for i in range(1, NR)] for f in range(FRONTS)]
+
+    def s_start(f):
+        start([s_cp[f][i - 1] for i in (2, 4, 6, 1)])
+
+    def s_pass(f):
+        for i in (2, 6, 4):
+            s_cp[f][i - 1].wait_recv()
+            s_cp[f][i].start()
+
+    def solve(f):
+        wait_recv([s_cp[f][i - 1] for i in (1, 3, 5, 7)])
+        left = s_all[:, f, :, 0:DEPTH].reshape(DEPTH, DEPTH)
+        right = s_all[:, f, :, DEPTH:].reshape(DEPTH, WIDTH)
+        sol[...] = lax.dot_general(
+            left, right, (((0,), (0,)), ((), ())), preferred_element_type=jnp.float32
+        ).astype(jnp.bfloat16)
+
     x_cp = [
         [
             remote(xs.at[n // 2, n % 2, i - 1], xr[n].at[i], x_ss.at[n, i], x_rs.at[n, i], row_to(i))
             for i in range(1, NR)
         ]
-        for n in range(2 * FRONTS)
+        for n in range(CHUNKS)
+    ]
+    x_cp += [
+        [
+            remote(
+                xs_wide.at[j, i - 1], last.at[j, i],
+                x_ss.at[CHUNKS + j, i], x_rs.at[CHUNKS + j, i], row_to(i),
+            )
+            for i in range(1, NR)
+        ]
+        for j in range(2)
     ]
 
     def side(e):
@@ -145,52 +174,74 @@
             )
             for e in range(1, 4 if f else NC)
         ]
-        for f in range(FRONTS)
+        for f in range(EARLY)
+    ]
+    g_cp += [
+        [
+            remote(
+                lower.at[EARLY], low_wide.at[c], g_ss.at[EARLY, e], g_rs.at[EARLY, e], col_to(e)
+            )
+            for e in range(1, NC)
+        ]
     ]
 
     def ring(f, s):
         block = low_all.at[f, pl.ds(lax.rem(z + s - 1, 4) * 4, 4)]
         return remote(block, block, z_ss.at[f, s], z_rs.at[f, s], col_to(NC - 4))
 
-    z_cp = [[ring(f, s) for s in range(1, 4)] if f else [] for f in range(FRONTS)]
+    z_cp = [[ring(f, s) for s in range(1, 4)] if f else [] for f in range(EARLY)]
 
     def y_parts(n):
+        if n == CHUNKS:
+            return (
+                lambda o: ys_wide.at[o - 1],
+                lambda o: yr_wide.at[pl.ds(o * 16, 16)],
+                relay_wide,
+            )
         f, h = n // 2, n % 2
         base, size = 2 * CUT[h], 2 * (CUT[h + 1] - CUT[h])
-        return f, h, pl.ds(base, size), lambda o: pl.ds(o * 2 * ROWS + base, size)
+        part = pl.ds(base, size)
+        return (
+            lambda o: ys.at[f, o - 1, part],
+            lambda o: yr[f].at[pl.ds(o * 2 * ROWS + base, size)],
+            relay.at[f, part],
+        )
 
     def y_copy(n, o):
-        f, h, src, dst = y_parts(n)
-        return remote(
-            ys.at[f, o - 1, src], yr[f].at[dst(o)], y_ss.at[n, o], y_rs.at[n, o], col_to(o)
-        )
+        src, dst, _ = y_parts(n)
+        return remote(src(o), dst(o), y_ss.at[n, o], y_rs.at[n, o], col_to(o))
 
     def relay_copy(n):
-        f, h, src, _ = y_parts(n)
-        return remote(
-            ys.at[f, 0, src], relay.at[f, src], y_ss.at[n, 1], q_rs.at[n], col_to(4)
-        )
+        src, _, way = y_parts(n)
+        return remote(src(1), way, y_ss.at[n, 1], q_rs.at[n], col_to(4))
 
     def forward_copy(n):
-        f, h, src, dst = y_parts(n)
-        return remote(
-            relay.at[f, src], yr[f].at[dst(1)], q_ss.at[n], y_rs.at[n, 1], col_to(NC - 3)
-        )
-
-    def own_copy(n):
-        f, h, src, _ = y_parts(n)
-        return pltpu.make_async_copy(own.at[src], last.at[src], own_sem.at[h])
+        _, dst, way = y_parts(n)
+        return remote(way, dst(1), q_ss.at[n], y_rs.at[n, 1], col_to(NC - 3))
+
+    def y_start(n, o):
+        if o == 1:
+            pl.when(edge)(lambda: relay_copy(n).start())
+            pl.when(jnp.logical_not(edge))(lambda: y_copy(n, 1).start())
+        else:
+            y_copy(n, o).start()
+
+    def own_copy(j):
+        return pltpu.make_async_copy(own.at[j], last.at[j, 0], own_sem.at[j])
 
     edge = y == 3
 
     pl.semaphore_wait(barrier, NR - 1 + NC - 1)
     start(m_cp)
+    s_start(EARLY)
+    start(g_cp[EARLY])
+    low_wide[c] = lower[EARLY]
     t_cp.wait()
-    for f in range(FRONTS):
+    for f in range(EARLY):
         for k in range(8):
             low[f, k] = lower[f, :, k * TILE:(k + 1) * TILE]
     for i in range(NR):
-        for f in range(FRONTS):
+        for f in range(EARLY):
             for j in range(2):
                 piece = low[f, tab_s[j * 8 + f, i]]
                 if i:
@@ -198,10 +249,10 @@
                 else:
                     lr[0, f, j] = piece
     start(l_cp)
-    start(s_cp[0])
+    s_start(0)
     pack_x(0)
     start(x_cp[0])
-    for f in range(FRONTS - 1):
+    for f in range(EARLY):
         yr[f][EMPTY] = jnp.zeros((TILE, TILE), jnp.bfloat16)
 
     wait_recv(m_cp)
@@ -226,7 +277,8 @@
                 m = map_s[i, f, k]
                 mine = lax.div(m, OWN_R) == r
                 q = jnp.where(rank == 0, q_first, q_second)
-                table = jnp.where(lane == jnp.where(mine, lax.rem(m, OWN_R), -1), q, table)
+                mark = q if f < EARLY else rank * 8 + i
+                table = jnp.where(lane == jnp.where(mine, lax.rem(m, OWN_R), -1), mark, table)
                 table = jnp.where(lane == jnp.where(mine, 32 + q, -1), rank * 8 + i, table)
                 q_first = q_first + jnp.where(mine & (rank == 0), 1, 0)
                 q_second = q_second + jnp.where(mine & (rank > 0), 1, 0)
@@ -245,6 +297,9 @@
                 at_place = jnp.where(mine, 64 + lax.rem(m, OWN_C), -1)
                 places = jnp.where(lane == at_place, o * 2 + rank, places)
                 rank = rank + jnp.where(mine, 1, 0)
+        if f == EARLY:
+            last_tab[...] = places
+            break
         tabv[16 + 8 * f:24 + 8 * f] = places
         r_cp = pltpu.make_async_copy(tabv.at[pl.ds(16 + 8 * f, 8)], rtab_s.at[f], loc.at[7])
         r_cp.start()
@@ -261,9 +316,35 @@
         lax.fori_loop(0, ROWS, take, 0)
         if f == 0:
             start(g_cp[0])
+            s_pass(EARLY)
+            s_pass(0)
+            solve(EARLY)
+            wait_recv(g_cp[EARLY])
+            upd_cp[EARLY].wait()
+
+            def subtract_wide(k, carry):
+                panel = low_wide[:, :, pl.ds(pl.multiple_of(k * TILE, TILE), TILE)]
+                product = lax.dot_general(
+                    panel.reshape(DEPTH, TILE), sol[...],
+                    (((0,), (0,)), ((), ())), preferred_element_type=jnp.float32,
+                )
+                rest = (upd[EARLY][k].astype(jnp.float32) - product).astype(jnp.bfloat16)
+                for t in range(4):
+                    comp[t, k] = rest[:, t * TILE:(t + 1) * TILE]
+                return carry
+
+            lax.fori_loop(0, 8, subtract_wide, 0)
+            for o in (1, 3, 2, 0):
+                for j in range(2):
+                    k = jnp.minimum(tab_s[j * 8 + EARLY, 16 + o], 3)
+                    if o:
+                        ys_wide[o - 1, j * 8:(j + 1) * 8] = comp[k, 0:8]
+                    else:
+                        yr_wide[j * 8:(j + 1) * 8] = comp[k, 0:8]
+                if o:
+                    y_start(CHUNKS, o)
             pack_x(1)
-    last_tab[...] = places
-    start(x_cp[1])
+            start(x_cp[1])
 
     def out_copy(p):
         return pltpu.make_async_copy(acc.at[p], early.at[p], o_sem.at[p])
@@ -282,7 +363,7 @@
                 tile = yr[f][jnp.where(held, at, EMPTY)]
                 cols = pl.ds(t * TILE, TILE)
                 acc[p, :, cols] = acc[p, :, cols] + tile.astype(jnp.float32)
-            if f == FRONTS - 2:
+            if f == EARLY - 1:
                 out_copy(p).start()
             return carry
 
@@ -298,25 +379,35 @@
             relay_copy(n).wait_recv()
             forward_copy(n).start()
 
-    for n in range(2 * FRONTS):
+    def pack_wide():
+        for o in range(1, REACH):
+            y_copy(CHUNKS, o).wait_recv()
+
+        for j in range(2):
+            def one(i, carry):
+                k = tab_s[j * 8 + EARLY, i + 1]
+                for t in range(2 * REACH):
+                    xs_wide[j, i, t] = yr_wide[t * 8 + k]
+                return carry
+
+            lax.fori_loop(0, NR - 1, one, 0)
+            k = tab_s[j * 8 + EARLY, 0]
+            for t in range(2 * REACH):
+                own[j, t] = yr_wide[t * 8 + k]
+            own_copy(j).start()
+
+    for n in range(CHUNKS):
         f, h = n // 2, n % 2
         low_q, high_q = CUT[h], CUT[h + 1]
         if h == 0:
-            wait_recv(s_cp[f])
-            left = s_all[:, f, :, 0:DEPTH].reshape(DEPTH, DEPTH)
-            right = s_all[:, f, :, DEPTH:].reshape(DEPTH, WIDTH)
-            sol[...] = lax.dot_general(
-                left, right, (((0,), (0,)), ((), ())), preferred_element_type=jnp.float32
-            ).astype(jnp.bfloat16)
+            solve(f)
             wait_recv(g_cp[0] if f == 0 else z_cp[f][2:])
         wait_recv(x_cp[n])
-        if n + 2 <= LAST:
-            if h == 0:
-                start(s_cp[f + 1])
-            start(x_cp[n + 2])
-        if n:
-            pass_on(n - 1)
-        if h == 0 and f + 1 < FRONTS:
+        if h == 0 and f + 1 < EARLY:
+            s_start(f + 1)
+        start(x_cp[n + 2])
+        pass_on(n - 1 if n else CHUNKS)
+        if h == 0 and f + 1 < EARLY:
             start(g_cp[f + 1])
 
         def subtract(q, carry):
@@ -342,45 +433,40 @@
                 at = 2 * low_q + j * size
                 if o:
                     ys[f, o - 1, at:at + size] = comp[k, low_q:high_q]
-                elif f == FRONTS - 1:
-                    own[at:at + size] = comp[k, low_q:high_q]
                 else:
                     yr[f][at:at + size] = comp[k, low_q:high_q]
-            if o == 1:
-                pl.when(edge)(lambda: relay_copy(n).start())
-                pl.when(jnp.logical_not(edge))(lambda: y_copy(n, 1).start())
-            elif o:
-                y_copy(n, o).start()
-            elif f == FRONTS - 1:
-                own_copy(n).start()
-        if f + 1 < FRONTS:
+            if o:
+                y_start(n, o)
+        if f + 1 < EARLY:
             if h == 0:
                 wait_recv(g_cp[f + 1])
                 z_cp[f + 1][0].start()
             else:
+                s_pass(f + 1)
                 z_cp[f + 1][0].wait_recv()
                 z_cp[f + 1][1].start()
-                if f + 2 < FRONTS:
+                if f + 2 < EARLY:
                     pack_x(f + 2)
                 z_cp[f + 1][1].wait_recv()
                 z_cp[f + 1][2].start()
-        if f >= 2 and h == 0:
-            if f == 2:
-                acc_cp.wait()
-            y_wait(2 * f - 4)
-            y_wait(2 * f - 3)
-            assemble(f - 2)
-    pass_on(LAST)
-    y_wait(LAST - 3)
-    y_wait(LAST - 2)
-    assemble(FRONTS - 2)
-    y_wait(LAST - 1)
-    y_wait(LAST)
-    own_copy(LAST - 1).wait()
-    own_copy(LAST).wait()
+        if n == CHUNKS - 3:
+            pack_wide()
+        if n == CHUNKS - 2:
+            acc_cp.wait()
+            y_wait(0)
+            y_wait(1)
+            assemble(0)
+    pass_on(CHUNKS - 1)
+    for f in range(1, EARLY):
+        y_wait(2 * f)
+        y_wait(2 * f + 1)
+        assemble(f)
+    for j in range(2):
+        wait_recv(x_cp[CHUNKS + j])
+        own_copy(j).wait()
     for cp in m_cp + l_cp + sum(s_cp + x_cp + g_cp + z_cp[1:], []):
         cp.wait_send()
-    for n in range(2 * FRONTS):
+    for n in range(CHUNKS + 1):
         for o in range(1, REACH):
             y_copy(n, o).wait_send()
         pl.when(edge)(lambda: forward_copy(n).wait_send())
@@ -413,18 +499,16 @@
 
             @pl.when(q >= 0)
             def _():
-                late = q >= CUT[1]
-                size = jnp.where(late, ROWS - CUT[1], CUT[1])
-                base = jnp.where(late, CUT[1], 0) + jnp.minimum(q, ROWS - 1)
+                source = jnp.minimum(q, 2 * NR - 1)
                 for t in range(OWN_C):
                     slot = tab[0, 64 + t]
 
                     @pl.when(slot >= 0)
                     def _():
                         place = jnp.minimum(slot, 2 * REACH - 1)
-                        at = lax.div(place, 2) * (2 * ROWS) + lax.rem(place, 2) * size + base
+                        tile = tiles[lax.div(source, NR), lax.rem(source, NR), place]
                         cols = pl.ds(t * TILE, TILE)
-                        held[p, :, cols] = held[p, :, cols] + tiles[at].astype(jnp.float32)
+                        held[p, :, cols] = held[p, :, cols] + tile.astype(jnp.float32)
 
             write(p).start()
 
@@ -441,6 +525,7 @@
 
 def per_device(pivot_inverse, upper, lower, update, row_map, column_map, parent):
     held = (OWN_R, TILE, OWN_C * TILE)
+    wide = (2, NR, 2 * REACH, TILE, TILE)
     dma = pltpu.SemaphoreType.DMA
     bf = jnp.bfloat16
     vmem = pl.BlockSpec(memory_space=pltpu.VMEM)
@@ -450,32 +535,37 @@
         kernel,
         out_shape=(
             jax.ShapeDtypeStruct(held, parent.dtype),
-            jax.ShapeDtypeStruct((EMPTY, TILE, TILE), bf),
+            jax.ShapeDtypeStruct(wide, bf),
             jax.ShapeDtypeStruct((8, 128), jnp.int32),
         ),
         in_specs=[scalars, scalars, vmem, vmem, vmem, anywhere, anywhere],
         out_specs=(anywhere, anywhere, vmem),
         scratch_shapes=[
             *[pltpu.VMEM((8, TILE, WIDTH), bf)] * FRONTS,
-            *[pltpu.VMEM((NR, TILE, WIDTH), bf)] * (2 * FRONTS),
-            *[pltpu.VMEM((EMPTY + 1, TILE, TILE), bf)] * (FRONTS - 1),
-            pltpu.VMEM((FRONTS, 8, LP, TILE), bf),
-            pltpu.VMEM((FRONTS, 2, NR - 1, TILE, WIDTH), bf),
-            pltpu.VMEM((NR - 1, FRONTS, 2, LP, TILE), bf),
-            pltpu.VMEM((NR, FRONTS, 2, LP, TILE), bf),
-            pltpu.VMEM((FRONTS, NC, ROWS, LP, TILE), bf),
+            *[pltpu.VMEM((NR, TILE, WIDTH), bf)] * CHUNKS,
+            *[pltpu.VMEM((EMPTY + 1, TILE, TILE), bf)] * EARLY,
+            pltpu.VMEM((EARLY, 8, LP, TILE), bf),
+            pltpu.VMEM((EARLY, 2, NR - 1, TILE, WIDTH), bf),
+            pltpu.VMEM((NR - 1, EARLY, 2, LP, TILE), bf),
+            pltpu.VMEM((NR, EARLY, 2, LP, TILE), bf),
+            pltpu.VMEM((EARLY, NC, ROWS, LP, TILE), bf),
+            pltpu.VMEM((NC, LP, 8 * TILE), bf),
             pltpu.VMEM((NR, FRONTS, UP, DEPTH + WIDTH), bf),
             pltpu.VMEM((DEPTH, WIDTH), bf),
             pltpu.VMEM((4, ROWS, TILE, TILE), bf),
-            pltpu.VMEM((FRONTS, REACH - 1, 2 * ROWS, TILE, TILE), bf),
-            pltpu.VMEM((2 * ROWS, TILE, TILE), bf),
-            pltpu.VMEM((FRONTS, 2 * ROWS, TILE, TILE), bf),
+            pltpu.VMEM((EARLY, REACH - 1, 2 * ROWS, TILE, TILE), bf),
+            pltpu.VMEM((EARLY, 2 * ROWS, TILE, TILE), bf),
+            pltpu.VMEM((REACH - 1, 16, TILE, TILE), bf),
+            pltpu.VMEM((REACH * 16, TILE, TILE), bf),
+            pltpu.VMEM((16, TILE, TILE), bf),
+            pltpu.VMEM((2, NR - 1, 2 * REACH, TILE, TILE), bf),
+            pltpu.VMEM((2, 2 * REACH, TILE, TILE), bf),
             pltpu.VMEM(held, parent.dtype),
             pltpu.VMEM((11, 8, 128), jnp.int32),
             pltpu.VMEM((48, 128), jnp.int32),
             pltpu.SMEM((11, 8, 128), jnp.int32),
             pltpu.SMEM((16, 128), jnp.int32),
-            pltpu.SMEM((FRONTS, 8, 128), jnp.int32),
+            pltpu.SMEM((EARLY, 8, 128), jnp.int32),
             dma((11,)), dma((11,)),
             dma((NR,)), dma((NR,)),
             dma((FRONTS, NR)), dma((FRONTS, NR)),
@@ -503,7 +593,7 @@
         out_specs=anywhere,
         scratch_shapes=[
             pltpu.VMEM(held, parent.dtype),
-            pltpu.VMEM((EMPTY, TILE, TILE), bf),
+            pltpu.VMEM(wide, bf),
             dma((OWN_R,)),
             dma,
             dma((OWN_R,)),

time: 172 us -> 172 us (level)
  no operation moved by 1% of the time
where the time goes in v3:
time: 172 us
  Pallas kernels  172 us (100%)
    pallas_call x1, Pallas kernels, per_device(): pl.pallas_call(kernel, out_shape=(jax.ShapeDtypeStruct(held, parent.dtype...  163 us
    pallas_call x1, Pallas kernels, per_device(): pl.pallas_call(finish, out_shape=jax.ShapeDtypeStruct(held, parent.dtype)...  8.59 us

profile of v3, /device:TPU:1, one launch (start us, length us, event | category | flops | bytes accessed | tf_op | source)
XLA Modules:
  0.0 171.8 jit_solution(7384697636267266358)
XLA Ops:
  0.0 163.2 %fronts.1 = (f32[16,128,1024]{2,1,0:T(8,128)}, bf16[2,8,8,128,128]{4,3,2,1,0:T(8,128)(2,1)}, s32[8,128]{1,0:T(8,128)}) custom-call(s32[4,8]{1,0:T(4,128)} %rows_s.1, s32[4,4]{1,0:T(4,128)} %cols_s.1, bf16[4,32,256]{2,1,0:T(8,128)(2,1)} %bitcast.6, bf16[4,32,512]{2,1,0:T(8,128)(2,1)} %upper.1, bf16[4,16,1024]{2,1,0:T(8,128)(2,1)} %lower.1, ...), custom_call_target="tpu_custom_call" | custom-call | tf_op jit(solution)/shard_map/fronts/pallas_call | solution.py:534
  163.2 8.6 %finish.1 = f32[16,128,1024]{2,1,0:T(8,128)} custom-call(s32[8,128]{1,0:T(8,128)} %get-tuple-element.8.tab, f32[16,128,1024]{2,1,0:T(8,128)} %get-tuple-element.9.early, bf16[2,8,8,128,128]{4,3,2,1,0:T(8,128)(2,1)} %get-tuple-element.10.last), custom_call_target="tpu_custom_call" | custom-call | tf_op jit(solution)/shard_map/finish/pallas_call | solution.py:589

commit v4 on v3

--- a/solution.py
+++ b/solution.py
@@ -32,7 +32,7 @@
     rows_s, cols_s, pivot, upper, lower, update, parent, early, last, last_tab,
     upd0, upd1, upd2, upd3, xr0, xr1, xr2, xr3, xr4, xr5, yr0, yr1, yr2,
     low, xs, ls, lr, low_all, low_wide, s_all, sol, comp, ys, relay,
-    ys_wide, yr_wide, relay_wide, xs_wide, own, acc,
+    ys_wide, yr_wide, relay_wide, half, half_wide, xs_wide, own, acc,
     mapv, tabv, map_s, tab_s, rtab_s,
     m_ss, m_rs, l_ss, l_rs, s_ss, s_rs, x_ss, x_rs, g_ss, g_rs, z_ss, z_rs,
     y_ss, y_rs, q_ss, q_rs, loc, own_sem, o_sem,
@@ -170,9 +170,9 @@
         [
             remote(
                 low_all.at[f, c], low_all.at[f, c], g_ss.at[f, e], g_rs.at[f, e],
-                side(e) if f else col_to(e),
+                side(e),
             )
-            for e in range(1, 4 if f else NC)
+            for e in range(1, 4)
         ]
         for f in range(EARLY)
     ]
@@ -189,47 +189,63 @@
         block = low_all.at[f, pl.ds(lax.rem(z + s - 1, 4) * 4, 4)]
         return remote(block, block, z_ss.at[f, s], z_rs.at[f, s], col_to(NC - 4))
 
-    z_cp = [[ring(f, s) for s in range(1, 4)] if f else [] for f in range(EARLY)]
+    z_cp = [[ring(f, s) for s in range(1, 4)] for f in range(EARLY)]
+
+    edge = y == 3
+    upper_half = y >= 2
 
     def y_parts(n):
         if n == CHUNKS:
             return (
-                lambda o: ys_wide.at[o - 1],
-                lambda o: yr_wide.at[pl.ds(o * 16, 16)],
+                lambda o, at, size: ys_wide.at[o - 1, pl.ds(at, size)],
+                lambda o, at, size: yr_wide.at[pl.ds(o * 16 + at, size)],
                 relay_wide,
+                half_wide,
+                8,
             )
         f, h = n // 2, n % 2
-        base, size = 2 * CUT[h], 2 * (CUT[h + 1] - CUT[h])
-        part = pl.ds(base, size)
+        base, size = 2 * CUT[h], CUT[h + 1] - CUT[h]
         return (
-            lambda o: ys.at[f, o - 1, part],
-            lambda o: yr[f].at[pl.ds(o * 2 * ROWS + base, size)],
-            relay.at[f, part],
+            lambda o, at, size: ys.at[f, o - 1, pl.ds(base + at, size)],
+            lambda o, at, size: yr[f].at[pl.ds(o * 2 * ROWS + base + at, size)],
+            relay.at[f, pl.ds(base, 2 * size)],
+            half.at[f, pl.ds(CUT[h], size)],
+            size,
         )
 
-    def y_copy(n, o):
-        src, dst, _ = y_parts(n)
-        return remote(src(o), dst(o), y_ss.at[n, o], y_rs.at[n, o], col_to(o))
-
-    def relay_copy(n):
-        src, _, way = y_parts(n)
-        return remote(src(1), way, y_ss.at[n, 1], q_rs.at[n], col_to(4))
-
-    def forward_copy(n):
-        _, dst, way = y_parts(n)
-        return remote(way, dst(1), q_ss.at[n], y_rs.at[n, 1], col_to(NC - 3))
+    def y_copy(n, m):
+        src, dst, _, _, size = y_parts(n)
+        o, at, length = (2, 0, size) if m == 0 else (2, size, size) if m == 2 else (m, 0, 2 * size)
+        return remote(
+            src(o, at, length), dst(o, at, length), y_ss.at[n, m], y_rs.at[n, m], col_to(o)
+        )
+
+    def relay_copy(n, m):
+        src, _, way, half_way, size = y_parts(n)
+        if m:
+            return remote(src(1, 0, 2 * size), way, y_ss.at[n, 1], q_rs.at[n, 1], col_to(4))
+        return remote(src(2, 0, size), half_way, y_ss.at[n, 0], q_rs.at[n, 0], col_to(4))
+
+    def forward_copy(n, m):
+        _, dst, way, half_way, size = y_parts(n)
+        if m:
+            return remote(
+                way, dst(1, 0, 2 * size), q_ss.at[n, 1], y_rs.at[n, 1], col_to(NC - 3)
+            )
+        return remote(half_way, dst(2, 0, size), q_ss.at[n, 0], y_rs.at[n, 0], col_to(NC - 2))
 
     def y_start(n, o):
-        if o == 1:
-            pl.when(edge)(lambda: relay_copy(n).start())
-            pl.when(jnp.logical_not(edge))(lambda: y_copy(n, 1).start())
-        else:
-            y_copy(n, o).start()
+        if o == 3:
+            y_copy(n, 3).start()
+            return
+        m, far = (1, edge) if o == 1 else (0, upper_half)
+        pl.when(far)(lambda: relay_copy(n, m).start())
+        pl.when(jnp.logical_not(far))(lambda: y_copy(n, m).start())
+        if o == 2:
+            y_copy(n, 2).start()
 
     def own_copy(j):
         return pltpu.make_async_copy(own.at[j], last.at[j, 0], own_sem.at[j])
-
-    edge = y == 3
 
     pl.semaphore_wait(barrier, NR - 1 + NC - 1)
     start(m_cp)
@@ -260,16 +276,7 @@
     map_cp.start()
     map_cp.wait()
 
-    for f in range(FRONTS):
-
-        def count(i, total):
-            held = jnp.int32(0)
-            for k in range(8):
-                held = held | jnp.where(lax.div(map_s[i, f, k], OWN_R) == r, 1, 0)
-            return total + held
-
-        heads = lax.fori_loop(0, NR, count, jnp.int32(0))
-
+    def make_table(f):
         def from_row(i, carry):
             table, q_first, q_second = carry
             rank = jnp.int32(0)
@@ -281,13 +288,13 @@
                 table = jnp.where(lane == jnp.where(mine, lax.rem(m, OWN_R), -1), mark, table)
                 table = jnp.where(lane == jnp.where(mine, 32 + q, -1), rank * 8 + i, table)
                 q_first = q_first + jnp.where(mine & (rank == 0), 1, 0)
-                q_second = q_second + jnp.where(mine & (rank > 0), 1, 0)
+                q_second = q_second - jnp.where(mine & (rank > 0), 1, 0)
                 rank = rank + jnp.where(mine, 1, 0)
             return table, q_first, q_second
 
         places, _, _ = lax.fori_loop(
             0, NR, from_row,
-            (jnp.full((8, 128), -1, jnp.int32), jnp.int32(0), jnp.maximum(heads, CUT[1])),
+            (jnp.full((8, 128), -1, jnp.int32), jnp.int32(0), jnp.int32(ROWS - 1)),
         )
         for o in range(REACH):
             rank = jnp.int32(0)
@@ -299,52 +306,61 @@
                 rank = rank + jnp.where(mine, 1, 0)
         if f == EARLY:
             last_tab[...] = places
-            break
+            return
         tabv[16 + 8 * f:24 + 8 * f] = places
         r_cp = pltpu.make_async_copy(tabv.at[pl.ds(16 + 8 * f, 8)], rtab_s.at[f], loc.at[7])
         r_cp.start()
         r_cp.wait()
 
-        if f == 0:
-            wait_recv(l_cp)
-
+    def take_panel(f):
         def take(q, carry):
             slot = jnp.clip(rtab_s[f, 0, 32 + q], 0, 15)
             low_all[f, c, q] = lr[lax.rem(slot, 8), f, lax.div(slot, 8)]
             return carry
 
         lax.fori_loop(0, ROWS, take, 0)
-        if f == 0:
-            start(g_cp[0])
-            s_pass(EARLY)
-            s_pass(0)
-            solve(EARLY)
-            wait_recv(g_cp[EARLY])
-            upd_cp[EARLY].wait()
-
-            def subtract_wide(k, carry):
-                panel = low_wide[:, :, pl.ds(pl.multiple_of(k * TILE, TILE), TILE)]
-                product = lax.dot_general(
-                    panel.reshape(DEPTH, TILE), sol[...],
-                    (((0,), (0,)), ((), ())), preferred_element_type=jnp.float32,
-                )
-                rest = (upd[EARLY][k].astype(jnp.float32) - product).astype(jnp.bfloat16)
-                for t in range(4):
-                    comp[t, k] = rest[:, t * TILE:(t + 1) * TILE]
-                return carry
-
-            lax.fori_loop(0, 8, subtract_wide, 0)
-            for o in (1, 3, 2, 0):
-                for j in range(2):
-                    k = jnp.minimum(tab_s[j * 8 + EARLY, 16 + o], 3)
-                    if o:
-                        ys_wide[o - 1, j * 8:(j + 1) * 8] = comp[k, 0:8]
-                    else:
-                        yr_wide[j * 8:(j + 1) * 8] = comp[k, 0:8]
-                if o:
-                    y_start(CHUNKS, o)
-            pack_x(1)
-            start(x_cp[1])
+
+    make_table(0)
+    wait_recv(l_cp)
+    take_panel(0)
+    start(g_cp[0])
+    s_pass(EARLY)
+    s_pass(0)
+    solve(EARLY)
+    wait_recv(g_cp[EARLY])
+    upd_cp[EARLY].wait()
+
+    def subtract_wide(k, carry):
+        panel = low_wide[:, :, pl.ds(pl.multiple_of(k * TILE, TILE), TILE)]
+        product = lax.dot_general(
+            panel.reshape(DEPTH, TILE), sol[...],
+            (((0,), (0,)), ((), ())), preferred_element_type=jnp.float32,
+        )
+        rest = (upd[EARLY][k].astype(jnp.float32) - product).astype(jnp.bfloat16)
+        for t in range(4):
+            comp[t, k] = rest[:, t * TILE:(t + 1) * TILE]
+        return carry
+
+    lax.fori_loop(0, 8, subtract_wide, 0)
+    for o in (1, 2, 3, 0):
+        for j in range(2):
+            k = jnp.minimum(tab_s[j * 8 + EARLY, 16 + o], 3)
+            if o:
+                ys_wide[o - 1, j * 8:(j + 1) * 8] = comp[k, 0:8]
+            else:
+                yr_wide[j * 8:(j + 1) * 8] = comp[k, 0:8]
+        if o:
+            y_start(CHUNKS, o)
+    wait_recv(g_cp[0])
+    z_cp[0][0].start()
+    make_table(1)
+    take_panel(1)
+    z_cp[0][0].wait_recv()
+    z_cp[0][1].start()
+    start(x_cp[1])
+    pack_x(1)
+    z_cp[0][1].wait_recv()
+    z_cp[0][2].start()
 
     def out_copy(p):
         return pltpu.make_async_copy(acc.at[p], early.at[p], o_sem.at[p])
@@ -370,18 +386,22 @@
         lax.fori_loop(0, OWN_R, one, 0)
 
     def y_wait(n):
-        for o in range(1, REACH):
-            y_copy(n, o).wait_recv()
+        for m in range(REACH):
+            y_copy(n, m).wait_recv()
 
     def pass_on(n):
         @pl.when(edge)
         def _():
-            relay_copy(n).wait_recv()
-            forward_copy(n).start()
+            relay_copy(n, 1).wait_recv()
+            forward_copy(n, 1).start()
+
+        @pl.when(upper_half)
+        def _():
+            relay_copy(n, 0).wait_recv()
+            forward_copy(n, 0).start()
 
     def pack_wide():
-        for o in range(1, REACH):
-            y_copy(CHUNKS, o).wait_recv()
+        y_wait(CHUNKS)
 
         for j in range(2):
             def one(i, carry):
@@ -401,12 +421,11 @@
         low_q, high_q = CUT[h], CUT[h + 1]
         if h == 0:
             solve(f)
-            wait_recv(g_cp[0] if f == 0 else z_cp[f][2:])
+            wait_recv(z_cp[f][2:])
         wait_recv(x_cp[n])
         if h == 0 and f + 1 < EARLY:
             s_start(f + 1)
         start(x_cp[n + 2])
-        pass_on(n - 1 if n else CHUNKS)
         if h == 0 and f + 1 < EARLY:
             start(g_cp[f + 1])
 
@@ -427,7 +446,7 @@
 
         lax.fori_loop(low_q, high_q, subtract, 0)
         size = high_q - low_q
-        for o in (1, 3, 2, 0):
+        for o in (1, 2, 3, 0):
             for j in range(2):
                 k = jnp.minimum(tab_s[j * 8 + f, 16 + o], 3)
                 at = 2 * low_q + j * size
@@ -437,6 +456,7 @@
                     yr[f][at:at + size] = comp[k, low_q:high_q]
             if o:
                 y_start(n, o)
+        pass_on(n - 1 if n else CHUNKS)
         if f + 1 < EARLY:
             if h == 0:
                 wait_recv(g_cp[f + 1])
@@ -449,8 +469,12 @@
                     pack_x(f + 2)
                 z_cp[f + 1][1].wait_recv()
                 z_cp[f + 1][2].start()
+        if n == 1:
+            make_table(2)
+            take_panel(2)
         if n == CHUNKS - 3:
             pack_wide()
+            make_table(EARLY)
         if n == CHUNKS - 2:
             acc_cp.wait()
             y_wait(0)
@@ -464,12 +488,13 @@
     for j in range(2):
         wait_recv(x_cp[CHUNKS + j])
         own_copy(j).wait()
-    for cp in m_cp + l_cp + sum(s_cp + x_cp + g_cp + z_cp[1:], []):
+    for cp in m_cp + l_cp + sum(s_cp + x_cp + g_cp + z_cp, []):
         cp.wait_send()
     for n in range(CHUNKS + 1):
-        for o in range(1, REACH):
-            y_copy(n, o).wait_send()
-        pl.when(edge)(lambda: forward_copy(n).wait_send())
+        for m in range(REACH):
+            y_copy(n, m).wait_send()
+        pl.when(edge)(lambda: forward_copy(n, 1).wait_send())
+        pl.when(upper_half)(lambda: forward_copy(n, 0).wait_send())
     for p in range(OWN_R):
         out_copy(p).wait()
 
@@ -478,40 +503,38 @@
     def read(p):
         return pltpu.make_async_copy(early.at[p], held.at[p], a_sem.at[p])
 
+    def read_tiles(p):
+        source = jnp.clip(tab[0, p], 0, 2 * NR - 1)
+        return pltpu.make_async_copy(
+            last.at[lax.div(source, NR), lax.rem(source, NR)], tiles.at[p], t_sem.at[p]
+        )
+
     def write(p):
         return pltpu.make_async_copy(held.at[p], out.at[p], o_sem.at[p])
 
     def reads(p, carry):
         read(p).start()
+        pl.when(tab[0, p] >= 0)(lambda: read_tiles(p).start())
         return carry
 
-    tiles_cp = pltpu.make_async_copy(last, tiles, t_sem)
-    tiles_cp.start()
     lax.fori_loop(0, OWN_R, reads, 0)
-    tiles_cp.wait()
 
     def one(p, carry):
-        q = tab[0, p]
-
-        @pl.when(p >= 0)
+        read(p).wait()
+
+        @pl.when(tab[0, p] >= 0)
         def _():
-            read(p).wait()
-
-            @pl.when(q >= 0)
-            def _():
-                source = jnp.minimum(q, 2 * NR - 1)
-                for t in range(OWN_C):
-                    slot = tab[0, 64 + t]
-
-                    @pl.when(slot >= 0)
-                    def _():
-                        place = jnp.minimum(slot, 2 * REACH - 1)
-                        tile = tiles[lax.div(source, NR), lax.rem(source, NR), place]
-                        cols = pl.ds(t * TILE, TILE)
-                        held[p, :, cols] = held[p, :, cols] + tile.astype(jnp.float32)
-
-            write(p).start()
-
+            read_tiles(p).wait()
+            for t in range(OWN_C):
+                slot = tab[0, 64 + t]
+
+                @pl.when(slot >= 0)
+                def _():
+                    tile = tiles[p, jnp.minimum(slot, 2 * REACH - 1)]
+                    cols = pl.ds(t * TILE, TILE)
+                    held[p, :, cols] = held[p, :, cols] + tile.astype(jnp.float32)
+
+        write(p).start()
         return carry
 
     lax.fori_loop(0, OWN_R, one, 0)
@@ -558,6 +581,8 @@
             pltpu.VMEM((REACH - 1, 16, TILE, TILE), bf),
             pltpu.VMEM((REACH * 16, TILE, TILE), bf),
             pltpu.VMEM((16, TILE, TILE), bf),
+            pltpu.VMEM((EARLY, ROWS, TILE, TILE), bf),
+            pltpu.VMEM((8, TILE, TILE), bf),
             pltpu.VMEM((2, NR - 1, 2 * REACH, TILE, TILE), bf),
             pltpu.VMEM((2, 2 * REACH, TILE, TILE), bf),
             pltpu.VMEM(held, parent.dtype),
@@ -573,7 +598,7 @@
             dma((FRONTS, NC)), dma((FRONTS, NC)),
             dma((FRONTS, 4)), dma((FRONTS, 4)),
             dma((2 * FRONTS, REACH)), dma((2 * FRONTS, REACH)),
-            dma((2 * FRONTS,)), dma((2 * FRONTS,)),
+            dma((2 * FRONTS, 2)), dma((2 * FRONTS, 2)),
             dma((8,)),
             dma((2,)),
             dma((OWN_R,)),
@@ -593,9 +618,9 @@
         out_specs=anywhere,
         scratch_shapes=[
             pltpu.VMEM(held, parent.dtype),
-            pltpu.VMEM(wide, bf),
+            pltpu.VMEM((OWN_R, *wide[2:]), bf),
             dma((OWN_R,)),
-            dma,
+            dma((OWN_R,)),
             dma((OWN_R,)),
         ],
         compiler_params=pltpu.CompilerParams(vmem_limit_bytes=60 * 1024 * 1024),

time: 172 us -> 161 us (0.936)
  Pallas kernels: 172 us -> 161 us
    pallas_call x1, Pallas kernels: 163 us -> 153 us  [per_device(): pl.pallas_call(kernel, out_shape=(jax.ShapeDtypeStruct(held, parent.dtype...]
where the time goes in v4:
time: 161 us
  Pallas kernels  161 us (100%)
    pallas_call x1, Pallas kernels, per_device(): pl.pallas_call(kernel, out_shape=(jax.ShapeDtypeStruct(held, parent.dtype...  153 us
    pallas_call x1, Pallas kernels, per_device(): pl.pallas_call(finish, out_shape=jax.ShapeDtypeStruct(held, parent.dtype)...  8.44 us

profile of v4, /device:TPU:1, one launch (start us, length us, event | category | flops | bytes accessed | tf_op | source)
XLA Modules:
  0.0 161.3 jit_solution(13250274955069729000)
XLA Ops:
  0.0 152.8 %fronts.1 = (f32[16,128,1024]{2,1,0:T(8,128)}, bf16[2,8,8,128,128]{4,3,2,1,0:T(8,128)(2,1)}, s32[8,128]{1,0:T(8,128)}) custom-call(s32[4,8]{1,0:T(4,128)} %rows_s.1, s32[4,4]{1,0:T(4,128)} %cols_s.1, bf16[4,32,256]{2,1,0:T(8,128)(2,1)} %bitcast.6, bf16[4,32,512]{2,1,0:T(8,128)(2,1)} %upper.1, bf16[4,16,1024]{2,1,0:T(8,128)(2,1)} %lower.1, ...), custom_call_target="tpu_custom_call" | custom-call | tf_op jit(solution)/shard_map/fronts/pallas_call | solution.py:557
  152.8 8.4 %finish.1 = f32[16,128,1024]{2,1,0:T(8,128)} custom-call(s32[8,128]{1,0:T(8,128)} %get-tuple-element.8.tab, f32[16,128,1024]{2,1,0:T(8,128)} %get-tuple-element.9.early, bf16[2,8,8,128,128]{4,3,2,1,0:T(8,128)(2,1)} %get-tuple-element.10.last), custom_call_target="tpu_custom_call" | custom-call | tf_op jit(solution)/shard_map/finish/pallas_call | solution.py:614

commit v5 on v4

--- a/solution.py
+++ b/solution.py
@@ -19,6 +19,7 @@
 CUT = (0, 4, 10)
 EARLY = FRONTS - 1
 CHUNKS = 2 * EARLY
+WIDE_EMPTY = 2 * NR * 2 * REACH
 DEPTH = 256
 LP = 16
 UP = 32
@@ -30,14 +31,14 @@
 
 def kernel(
     rows_s, cols_s, pivot, upper, lower, update, parent, early, last, last_tab,
-    upd0, upd1, upd2, upd3, xr0, xr1, xr2, xr3, xr4, xr5, yr0, yr1, yr2,
+    upd0, upd1, upd2, upd3, xr0, xr1, xr2, xr3, xr4, xr5, yr0, yr1,
     low, xs, ls, lr, low_all, low_wide, s_all, sol, comp, ys, relay,
-    ys_wide, yr_wide, relay_wide, half, half_wide, xs_wide, own, acc,
+    ys_wide, yr_wide, relay_wide, half, half_wide, xs_wide, xr_wide, own, acc,
     mapv, tabv, map_s, tab_s, rtab_s,
     m_ss, m_rs, l_ss, l_rs, s_ss, s_rs, x_ss, x_rs, g_ss, g_rs, z_ss, z_rs,
     y_ss, y_rs, q_ss, q_rs, loc, own_sem, o_sem,
 ):
-    upd, yr = (upd0, upd1, upd2, upd3), (yr0, yr1, yr2)
+    upd, yr = (upd0, upd1, upd2, upd3), (yr0, yr1, last)
     xr = (xr0, xr1, xr2, xr3, xr4, xr5)
     r = lax.axis_index("prow")
     c = lax.axis_index("pcol")
@@ -155,7 +156,7 @@
     x_cp += [
         [
             remote(
-                xs_wide.at[j, i - 1], last.at[j, i],
+                xs_wide.at[j, i - 1], xr_wide.at[pl.ds((j * NR + i) * 8, 8)],
                 x_ss.at[CHUNKS + j, i], x_rs.at[CHUNKS + j, i], row_to(i),
             )
             for i in range(1, NR)
@@ -239,13 +240,18 @@
             y_copy(n, 3).start()
             return
         m, far = (1, edge) if o == 1 else (0, upper_half)
+        if o == 2 and n == CHUNKS - 1:
+            y_copy(n, 0).start()
+            y_copy(n, 2).start()
+            return
         pl.when(far)(lambda: relay_copy(n, m).start())
         pl.when(jnp.logical_not(far))(lambda: y_copy(n, m).start())
         if o == 2:
             y_copy(n, 2).start()
 
-    def own_copy(j):
-        return pltpu.make_async_copy(own.at[j], last.at[j, 0], own_sem.at[j])
+    def own_copy(h):
+        part = pl.ds(2 * CUT[h], 2 * (CUT[h + 1] - CUT[h]))
+        return pltpu.make_async_copy(own.at[part], last.at[part], own_sem.at[h])
 
     pl.semaphore_wait(barrier, NR - 1 + NC - 1)
     start(m_cp)
@@ -268,12 +274,14 @@
     s_start(0)
     pack_x(0)
     start(x_cp[0])
-    for f in range(EARLY):
+    for f in range(EARLY - 1):
         yr[f][EMPTY] = jnp.zeros((TILE, TILE), jnp.bfloat16)
+    xr_wide[WIDE_EMPTY] = jnp.zeros((TILE, TILE), jnp.bfloat16)
 
     wait_recv(m_cp)
     map_cp = pltpu.make_async_copy(mapv, map_s, loc.at[6])
     map_cp.start()
+    s_pass(EARLY)
     map_cp.wait()
 
     def make_table(f):
@@ -304,9 +312,8 @@
                 at_place = jnp.where(mine, 64 + lax.rem(m, OWN_C), -1)
                 places = jnp.where(lane == at_place, o * 2 + rank, places)
                 rank = rank + jnp.where(mine, 1, 0)
-        if f == EARLY:
+        if f == EARLY - 1:
             last_tab[...] = places
-            return
         tabv[16 + 8 * f:24 + 8 * f] = places
         r_cp = pltpu.make_async_copy(tabv.at[pl.ds(16 + 8 * f, 8)], rtab_s.at[f], loc.at[7])
         r_cp.start()
@@ -324,8 +331,6 @@
     wait_recv(l_cp)
     take_panel(0)
     start(g_cp[0])
-    s_pass(EARLY)
-    s_pass(0)
     solve(EARLY)
     wait_recv(g_cp[EARLY])
     upd_cp[EARLY].wait()
@@ -351,6 +356,7 @@
                 yr_wide[j * 8:(j + 1) * 8] = comp[k, 0:8]
         if o:
             y_start(CHUNKS, o)
+    s_pass(0)
     wait_recv(g_cp[0])
     z_cp[0][0].start()
     make_table(1)
@@ -379,8 +385,21 @@
                 tile = yr[f][jnp.where(held, at, EMPTY)]
                 cols = pl.ds(t * TILE, TILE)
                 acc[p, :, cols] = acc[p, :, cols] + tile.astype(jnp.float32)
-            if f == EARLY - 1:
-                out_copy(p).start()
+            return carry
+
+        lax.fori_loop(0, OWN_R, one, 0)
+
+    def assemble_wide():
+        def one(p, carry):
+            source = rtab_s[EARLY, 0, p]
+            for t in range(OWN_C):
+                slot = rtab_s[EARLY, 0, 64 + t]
+                held = (source >= 0) & (slot >= 0)
+                at = jnp.clip(source, 0, 15) * 8 + jnp.clip(slot, 0, 7)
+                tile = xr_wide[jnp.where(held, at, WIDE_EMPTY)]
+                cols = pl.ds(t * TILE, TILE)
+                acc[p, :, cols] = acc[p, :, cols] + tile.astype(jnp.float32)
+            out_copy(p).start()
             return carry
 
         lax.fori_loop(0, OWN_R, one, 0)
@@ -394,6 +413,9 @@
         def _():
             relay_copy(n, 1).wait_recv()
             forward_copy(n, 1).start()
+
+        if n == CHUNKS - 1:
+            return
 
         @pl.when(upper_half)
         def _():
@@ -413,9 +435,9 @@
             lax.fori_loop(0, NR - 1, one, 0)
             k = tab_s[j * 8 + EARLY, 0]
             for t in range(2 * REACH):
-                own[j, t] = yr_wide[t * 8 + k]
-            own_copy(j).start()
-
+                xr_wide[j * NR * 8 + t] = yr_wide[t * 8 + k]
+
+    pass_on(CHUNKS)
     for n in range(CHUNKS):
         f, h = n // 2, n % 2
         low_q, high_q = CUT[h], CUT[h + 1]
@@ -452,11 +474,16 @@
                 at = 2 * low_q + j * size
                 if o:
                     ys[f, o - 1, at:at + size] = comp[k, low_q:high_q]
+                elif f == EARLY - 1:
+                    own[at:at + size] = comp[k, low_q:high_q]
                 else:
                     yr[f][at:at + size] = comp[k, low_q:high_q]
             if o:
                 y_start(n, o)
-        pass_on(n - 1 if n else CHUNKS)
+            elif f == EARLY - 1:
+                own_copy(h).start()
+        if n:
+            pass_on(n - 1)
         if f + 1 < EARLY:
             if h == 0:
                 wait_recv(g_cp[f + 1])
@@ -475,26 +502,26 @@
         if n == CHUNKS - 3:
             pack_wide()
             make_table(EARLY)
-        if n == CHUNKS - 2:
-            acc_cp.wait()
-            y_wait(0)
-            y_wait(1)
-            assemble(0)
     pass_on(CHUNKS - 1)
-    for f in range(1, EARLY):
+    acc_cp.wait()
+    for f in range(EARLY - 1):
         y_wait(2 * f)
         y_wait(2 * f + 1)
         assemble(f)
     for j in range(2):
         wait_recv(x_cp[CHUNKS + j])
-        own_copy(j).wait()
+    assemble_wide()
+    for h in range(2):
+        y_wait(CHUNKS - 2 + h)
+        own_copy(h).wait()
     for cp in m_cp + l_cp + sum(s_cp + x_cp + g_cp + z_cp, []):
         cp.wait_send()
     for n in range(CHUNKS + 1):
         for m in range(REACH):
             y_copy(n, m).wait_send()
         pl.when(edge)(lambda: forward_copy(n, 1).wait_send())
-        pl.when(upper_half)(lambda: forward_copy(n, 0).wait_send())
+        if n != CHUNKS - 1:
+            pl.when(upper_half)(lambda: forward_copy(n, 0).wait_send())
     for p in range(OWN_R):
         out_copy(p).wait()
 
@@ -503,34 +530,35 @@
     def read(p):
         return pltpu.make_async_copy(early.at[p], held.at[p], a_sem.at[p])
 
-    def read_tiles(p):
-        source = jnp.clip(tab[0, p], 0, 2 * NR - 1)
-        return pltpu.make_async_copy(
-            last.at[lax.div(source, NR), lax.rem(source, NR)], tiles.at[p], t_sem.at[p]
-        )
-
     def write(p):
         return pltpu.make_async_copy(held.at[p], out.at[p], o_sem.at[p])
 
     def reads(p, carry):
         read(p).start()
-        pl.when(tab[0, p] >= 0)(lambda: read_tiles(p).start())
         return carry
 
+    tiles_cp = pltpu.make_async_copy(last, tiles, t_sem)
+    tiles_cp.start()
     lax.fori_loop(0, OWN_R, reads, 0)
+    tiles_cp.wait()
 
     def one(p, carry):
         read(p).wait()
 
         @pl.when(tab[0, p] >= 0)
         def _():
-            read_tiles(p).wait()
+            q = jnp.minimum(tab[0, p], ROWS - 1)
+            late = q >= CUT[1]
+            size = jnp.where(late, ROWS - CUT[1], CUT[1])
+            base = jnp.where(late, CUT[1], 0) + q
             for t in range(OWN_C):
                 slot = tab[0, 64 + t]
 
                 @pl.when(slot >= 0)
                 def _():
-                    tile = tiles[p, jnp.minimum(slot, 2 * REACH - 1)]
+                    place = jnp.minimum(slot, 2 * REACH - 1)
+                    at = lax.div(place, 2) * (2 * ROWS) + lax.rem(place, 2) * size + base
+                    tile = tiles[at]
                     cols = pl.ds(t * TILE, TILE)
                     held[p, :, cols] = held[p, :, cols] + tile.astype(jnp.float32)
 
@@ -548,7 +576,6 @@
 
 def per_device(pivot_inverse, upper, lower, update, row_map, column_map, parent):
     held = (OWN_R, TILE, OWN_C * TILE)
-    wide = (2, NR, 2 * REACH, TILE, TILE)
     dma = pltpu.SemaphoreType.DMA
     bf = jnp.bfloat16
     vmem = pl.BlockSpec(memory_space=pltpu.VMEM)
@@ -558,7 +585,7 @@
         kernel,
         out_shape=(
             jax.ShapeDtypeStruct(held, parent.dtype),
-            jax.ShapeDtypeStruct(wide, bf),
+            jax.ShapeDtypeStruct((EMPTY, TILE, TILE), bf),
             jax.ShapeDtypeStruct((8, 128), jnp.int32),
         ),
         in_specs=[scalars, scalars, vmem, vmem, vmem, anywhere, anywhere],
@@ -566,7 +593,7 @@
         scratch_shapes=[
             *[pltpu.VMEM((8, TILE, WIDTH), bf)] * FRONTS,
             *[pltpu.VMEM((NR, TILE, WIDTH), bf)] * CHUNKS,
-            *[pltpu.VMEM((EMPTY + 1, TILE, TILE), bf)] * EARLY,
+            *[pltpu.VMEM((EMPTY + 1, TILE, TILE), bf)] * (EARLY - 1),
             pltpu.VMEM((EARLY, 8, LP, TILE), bf),
             pltpu.VMEM((EARLY, 2, NR - 1, TILE, WIDTH), bf),
             pltpu.VMEM((NR - 1, EARLY, 2, LP, TILE), bf),
@@ -584,13 +611,14 @@
             pltpu.VMEM((EARLY, ROWS, TILE, TILE), bf),
             pltpu.VMEM((8, TILE, TILE), bf),
             pltpu.VMEM((2, NR - 1, 2 * REACH, TILE, TILE), bf),
-            pltpu.VMEM((2, 2 * REACH, TILE, TILE), bf),
+            pltpu.VMEM((WIDE_EMPTY + 1, TILE, TILE), bf),
+            pltpu.VMEM((2 * ROWS, TILE, TILE), bf),
             pltpu.VMEM(held, parent.dtype),
             pltpu.VMEM((11, 8, 128), jnp.int32),
             pltpu.VMEM((48, 128), jnp.int32),
             pltpu.SMEM((11, 8, 128), jnp.int32),
             pltpu.SMEM((16, 128), jnp.int32),
-            pltpu.SMEM((EARLY, 8, 128), jnp.int32),
+            pltpu.SMEM((FRONTS, 8, 128), jnp.int32),
             dma((11,)), dma((11,)),
             dma((NR,)), dma((NR,)),
             dma((FRONTS, NR)), dma((FRONTS, NR)),
@@ -618,9 +646,9 @@
         out_specs=anywhere,
         scratch_shapes=[
             pltpu.VMEM(held, parent.dtype),
-            pltpu.VMEM((OWN_R, *wide[2:]), bf),
+            pltpu.VMEM((EMPTY, TILE, TILE), bf),
             dma((OWN_R,)),
-            dma((OWN_R,)),
+            dma,
             dma((OWN_R,)),
         ],
         compiler_params=pltpu.CompilerParams(vmem_limit_bytes=60 * 1024 * 1024),

time: 161 us -> 160 us (level)
  no operation moved by 1% of the time
where the time goes in v5:
time: 160 us
  Pallas kernels  160 us (100%)
    pallas_call x1, Pallas kernels, per_device(): pl.pallas_call(kernel, out_shape=(jax.ShapeDtypeStruct(held, parent.dtype...  152 us
    pallas_call x1, Pallas kernels, per_device(): pl.pallas_call(finish, out_shape=jax.ShapeDtypeStruct(held, parent.dtype)...  8.23 us

profile of v5, /device:TPU:1, one launch (start us, length us, event | category | flops | bytes accessed | tf_op | source)
XLA Modules:
  0.0 160.0 jit_solution(14643936444632032121)
XLA Ops:
  0.0 151.8 %fronts.1 = (f32[16,128,1024]{2,1,0:T(8,128)}, bf16[80,128,128]{2,1,0:T(8,128)(2,1)}, s32[8,128]{1,0:T(8,128)}) custom-call(s32[4,8]{1,0:T(4,128)} %rows_s.1, s32[4,4]{1,0:T(4,128)} %cols_s.1, bf16[4,32,256]{2,1,0:T(8,128)(2,1)} %bitcast.6, bf16[4,32,512]{2,1,0:T(8,128)(2,1)} %upper.1, bf16[4,16,1024]{2,1,0:T(8,128)(2,1)} %lower.1, ...), custom_call_target="tpu_custom_call" | custom-call | tf_op jit(solution)/shard_map/fronts/pallas_call | solution.py:584
  151.8 8.2 %finish.1 = f32[16,128,1024]{2,1,0:T(8,128)} custom-call(s32[8,128]{1,0:T(8,128)} %get-tuple-element.8.tab, f32[16,128,1024]{2,1,0:T(8,128)} %get-tuple-element.9.early, bf16[80,128,128]{2,1,0:T(8,128)(2,1)} %get-tuple-element.10.last), custom_call_target="tpu_custom_call" | custom-call | tf_op jit(solution)/shard_map/finish/pallas_call | solution.py:642

commit v6 on v5

--- a/solution.py
+++ b/solution.py
@@ -240,7 +240,7 @@
             y_copy(n, 3).start()
             return
         m, far = (1, edge) if o == 1 else (0, upper_half)
-        if o == 2 and n == CHUNKS - 1:
+        if o == 2 and CHUNKS - 2 <= n < CHUNKS:
             y_copy(n, 0).start()
             y_copy(n, 2).start()
             return
@@ -414,7 +414,7 @@
             relay_copy(n, 1).wait_recv()
             forward_copy(n, 1).start()
 
-        if n == CHUNKS - 1:
+        if CHUNKS - 2 <= n < CHUNKS:
             return
 
         @pl.when(upper_half)
@@ -520,7 +520,7 @@
         for m in range(REACH):
             y_copy(n, m).wait_send()
         pl.when(edge)(lambda: forward_copy(n, 1).wait_send())
-        if n != CHUNKS - 1:
+        if not CHUNKS - 2 <= n < CHUNKS:
             pl.when(upper_half)(lambda: forward_copy(n, 0).wait_send())
     for p in range(OWN_R):
         out_copy(p).wait()
@@ -540,13 +540,22 @@
     tiles_cp = pltpu.make_async_copy(last, tiles, t_sem)
     tiles_cp.start()
     lax.fori_loop(0, OWN_R, reads, 0)
+
+    def plain(p, carry):
+        @pl.when(tab[0, p] < 0)
+        def _():
+            read(p).wait()
+            write(p).start()
+
+        return carry
+
+    lax.fori_loop(0, OWN_R, plain, 0)
     tiles_cp.wait()
 
     def one(p, carry):
-        read(p).wait()
-
         @pl.when(tab[0, p] >= 0)
         def _():
+            read(p).wait()
             q = jnp.minimum(tab[0, p], ROWS - 1)
             late = q >= CUT[1]
             size = jnp.where(late, ROWS - CUT[1], CUT[1])
@@ -562,7 +571,8 @@
                     cols = pl.ds(t * TILE, TILE)
                     held[p, :, cols] = held[p, :, cols] + tile.astype(jnp.float32)
 
-        write(p).start()
+            write(p).start()
+
         return carry
 
     lax.fori_loop(0, OWN_R, one, 0)

time: 160 us -> 160 us (level)
  no operation moved by 1% of the time
where the time goes in v6:
time: 160 us
  Pallas kernels  160 us (100%)
    pallas_call x1, Pallas kernels, per_device(): pl.pallas_call(kernel, out_shape=(jax.ShapeDtypeStruct(held, parent.dtype...  152 us
    pallas_call x1, Pallas kernels, per_device(): pl.pallas_call(finish, out_shape=jax.ShapeDtypeStruct(held, parent.dtype)...  7.87 us

profile of v6, /device:TPU:1, one launch (start us, length us, event | category | flops | bytes accessed | tf_op | source)
XLA Modules:
  0.0 159.6 jit_solution(8055320279541941517)
XLA Ops:
  0.0 151.8 %fronts.1 = (f32[16,128,1024]{2,1,0:T(8,128)}, bf16[80,128,128]{2,1,0:T(8,128)(2,1)}, s32[8,128]{1,0:T(8,128)}) custom-call(s32[4,8]{1,0:T(4,128)} %rows_s.1, s32[4,4]{1,0:T(4,128)} %cols_s.1, bf16[4,32,256]{2,1,0:T(8,128)(2,1)} %bitcast.6, bf16[4,32,512]{2,1,0:T(8,128)(2,1)} %upper.1, bf16[4,16,1024]{2,1,0:T(8,128)(2,1)} %lower.1, ...), custom_call_target="tpu_custom_call" | custom-call | tf_op jit(solution)/shard_map/fronts/pallas_call | solution.py:594
  151.8 7.9 %finish.1 = f32[16,128,1024]{2,1,0:T(8,128)} custom-call(s32[8,128]{1,0:T(8,128)} %get-tuple-element.8.tab, f32[16,128,1024]{2,1,0:T(8,128)} %get-tuple-element.9.early, bf16[80,128,128]{2,1,0:T(8,128)(2,1)} %get-tuple-element.10.last), custom_call_target="tpu_custom_call" | custom-call | tf_op jit(solution)/shard_map/finish/pallas_call | solution.py:652
